TPU v7x, 32 devices: a whole 2x2x4 slice. The times are simulated.
32 devices in a mesh: gx: 2 (over x), gy: 4 (over y, core), gz: 4 (over z).
Axes of the slice: x: 2, y: 2, z: 4, core: 2. Of those that a mesh axis runs over, the one named last changes fastest.
Arguments:
- source: float32 [32, 128, 512], P('gx', 'gy', 'gz'), may hold values from -24 to 24
- conductivity: float32 [32, 128, 512], P('gx', 'gy', 'gz'), may hold values from 0.5 to 8
Outputs:
- correction: float32 [32, 128, 512], P('gx', 'gy', 'gz')
All inputs are finite; a program needn't handle non-finite values.
Results may differ from a plain program's by a relative error of at most 0.0001.
Values sent between devices are 32-bit elements; how exact they have to be, the bound alone decides.
No kernel may reach another device: no remote copies, remote signals or barrier semaphores. Data moves between devices by JAX's collectives and lax.ppermute only.
A program may use at most 128 MiB of HBM per device.

v0:
```python
import jax
import jax.numpy as jnp
from jax import lax
from jax.sharding import PartitionSpec as P

SWEEPS = 6
COARSE_SWEEPS = 16


DAMPING = 0.8


def with_halo(array, sides, width):
    for axis, dim in sides:
        size, length = (lax.axis_size(axis), array.shape[dim])
        up = [(i, (i + 1) % size) for i in range(size - 1)]
        down = [(j, i) for i, j in up]
        last = lax.slice_in_dim(array, length - width, length, axis=dim)
        first = lax.slice_in_dim(array, 0, width, axis=dim)
        before = lax.ppermute(last, axis, up)
        after = lax.ppermute(first, axis, down)
        array = jnp.concatenate([before, array, after], axis=dim)
    return array


def centre(padded):
    return padded[1:-1, 1:-1, 1:-1]


def neighbours(padded):
    return [
        padded[2:, 1:-1, 1:-1],
        padded[:-2, 1:-1, 1:-1],
        padded[1:-1, 2:, 1:-1],
        padded[1:-1, :-2, 1:-1],
        padded[1:-1, 1:-1, 2:],
        padded[1:-1, 1:-1, :-2],
    ]


def zero_pad(field):
    return jnp.pad(field, 1)


def stencil(field_pad, coef_pad, weight):
    middle = centre(field_pad)
    coef_mid = centre(coef_pad)
    total = jnp.zeros_like(middle)
    for field_near, coef_near in zip(neighbours(field_pad), neighbours(coef_pad)):
        total = total + 0.5 * (coef_mid + coef_near) * (middle - field_near)
    return weight * total


def diagonal(coef_pad, weight):
    coef_mid = centre(coef_pad)
    total = jnp.zeros_like(coef_mid)
    for coef_near in neighbours(coef_pad):
        total = total + 0.5 * (coef_mid + coef_near)
    return weight * total


def restrict(field):
    shape = field.shape
    blocks = field.reshape(shape[0] // 2, 2, shape[1] // 2, 2, shape[2] // 2, 2)
    return blocks.mean(axis=(1, 3, 5))


def prolong(field):
    return jnp.repeat(jnp.repeat(jnp.repeat(field, 2, 0), 2, 1), 2, 2)


def jacobi(field, rhs_level, coef_pad, diag_terms, weight, padder):
    return field + DAMPING * (rhs_level - stencil(padder(field), coef_pad, weight)) / diag_terms


def face_rim(field):
    return with_halo(field, (("gx", 0), ("gy", 1), ("gz", 2)), 1)


def slab_pad(field):
    extended = with_halo(field, (("gx", 0),), 1)
    return jnp.pad(extended, ((0, 0), (1, 1), (1, 1)))


def single_sweeps(field, rhs_level, coef_pad, diag_terms, weight):
    for sweep_index in range(SWEEPS):
        field = jacobi(field, rhs_level, coef_pad, diag_terms, weight, face_rim)
    return field


def coarse_solve(rhs_level, coef_level):
    weight = 0.25**4
    coef_pad = zero_pad(coef_level)
    diag_terms = diagonal(coef_pad, weight)

    def coarse_step(count, field):
        return jacobi(field, rhs_level, coef_pad, diag_terms, weight, zero_pad)

    return lax.fori_loop(0, COARSE_SWEEPS, coarse_step, jnp.zeros_like(rhs_level))


def level_three(rhs_level, coef_level, padder, lower_solve):
    weight = 0.25**3
    coef_pad = padder(coef_level)
    diag_terms = diagonal(coef_pad, weight)
    field = jnp.zeros_like(rhs_level)
    for sweep_index in range(SWEEPS):
        field = jacobi(field, rhs_level, coef_pad, diag_terms, weight, padder)
    residual = rhs_level - stencil(padder(field), coef_pad, weight)
    field = field + prolong(lower_solve(restrict(residual), restrict(coef_level)))
    for sweep_index in range(SWEEPS):
        field = jacobi(field, rhs_level, coef_pad, diag_terms, weight, padder)
    return field


def shards(source, conductivity):
    count_x, count_y, count_z = (lax.axis_size("gx"), lax.axis_size("gy"), lax.axis_size("gz"))
    place_x, place_y, place_z = (lax.axis_index("gx"), lax.axis_index("gy"), lax.axis_index("gz"))
    rhs_level = source
    coef_level = conductivity
    saved = []
    for level_index in range(3):
        weight = 0.25**level_index
        coef_pad = face_rim(coef_level)
        diag_terms = diagonal(coef_pad, weight)
        extras = None
        field = single_sweeps(jnp.zeros_like(rhs_level), rhs_level, coef_pad, diag_terms, weight)
        residual = rhs_level - stencil(face_rim(field), coef_pad, weight)
        saved.append((field, rhs_level, coef_pad, diag_terms, weight, extras))
        rhs_level = restrict(residual)
        coef_level = restrict(coef_level)
    rows_x, rows_y, rows_z = rhs_level.shape
    stacked = jnp.stack([rhs_level, coef_level])[None]
    gathered = lax.all_gather(stacked, ("gy", "gz"), axis=0, tiled=True)
    slab = gathered.reshape(count_y, count_z, 2, rows_x, rows_y, rows_z)
    slab = slab.transpose(2, 3, 0, 4, 1, 5).reshape(2, rows_x, count_y * rows_y, count_z * rows_z)

    def lower_groups(rhs_low, coef_low):
        lowered = lax.all_gather(jnp.stack([rhs_low, coef_low]), "gx", axis=1, tiled=True)
        whole = coarse_solve(lowered[0], lowered[1])
        return lax.dynamic_slice_in_dim(whole, place_x * (rows_x // 2), rows_x // 2, 0)

    field = level_three(slab[0], slab[1], slab_pad, lower_groups)
    field = lax.dynamic_slice_in_dim(field, place_y * rows_y, rows_y, 1)
    result = lax.dynamic_slice_in_dim(field, place_z * rows_z, rows_z, 2)
    for level_index in (2, 1, 0):
        field, rhs_here, coef_pad, diag_terms, weight, extras = saved[level_index]
        field = field + prolong(result)
        field = single_sweeps(field, rhs_here, coef_pad, diag_terms, weight)
        result = field
    return result


def solution(mesh):
    in_specs = (P("gx", "gy", "gz"), P("gx", "gy", "gz"))
    out_specs = P("gx", "gy", "gz")
    return jax.shard_map(shards, mesh=mesh, in_specs=in_specs, out_specs=out_specs, check_vma=False)
```

profile of v0, /device:TPU:30, one launch (start us, length us, event | category | flops | bytes accessed | tf_op | source)
XLA Modules:
  0.0 1191.4 jit_solution(3135257969433478578)
XLA Ops:
  2.1 4.5 collective-permute-start.1
  7.9 4.5 collective-permute-start
  25.0 4.6 collective-permute-start.8
  31.1 4.6 collective-permute-start.9
  38.2 4.5 collective-permute-done.11
  51.4 4.2 collective-permute-done.13
  69.5 4.8 collective-permute-done.16
  83.5 4.2 collective-permute-done.19
  98.7 5.1 collective-permute-done.22
  111.5 4.2 collective-permute-done.25
  126.7 5.1 collective-permute-done.28
  139.4 4.5 collective-permute-start.49
  145.2 18.1 %reshape.112 = f32[8,2,16,2,64,2]{5,4,3,2,1,0:T(8,128)} reshape(f32[16,32,128]{2,1,0:T(8,128)S(1)} %copy-done) | data formatting | bytes 524288 | tf_op jit(solution)/shard_map/reshape | solution.py:64
  163.4 7.0 reduce_sum.87
  181.2 4.5 collective-permute-start.48
  190.9 4.5 collective-permute-start.36
  216.1 4.8 collective-permute-done.40
  225.5 4.4 collective-permute-start.42
  235.6 4.3 collective-permute-start.44
  245.1 4.3 collective-permute-start.46
  251.7 4.5 collective-permute-start.57
  261.3 18.1 %reshape.111 = f32[8,2,16,2,64,2]{5,4,3,2,1,0:T(8,128)} reshape(f32[16,32,128]{2,1,0:T(8,128)S(1)} %fusion.163) | data formatting | bytes 524288 | tf_op jit(solution)/shard_map/reshape | solution.py:64
  279.5 7.0 reduce_sum.86
  288.4 4.3 collective-permute-start.60
  315.7 4.4 collective-permute-done.65
  320.2 4.5 collective-permute-start.66
  326.0 4.5 collective-permute-start.96
  350.0 4.5 collective-permute-start.72
  370.2 4.6 collective-permute-start.76
  377.1 4.4 collective-permute-done.77
  400.1 4.5 collective-permute-start.104
  420.4 4.6 collective-permute-start.88
  427.3 4.4 collective-permute-done.89
  452.1 4.4 collective-permute-done.95
  462.1 4.5 collective-permute-start.108
  482.7 4.2 collective-permute-done.113
  504.8 4.2 collective-permute-done.119
  526.9 4.2 collective-permute-done.125
  549.0 4.2 collective-permute-done.131
  571.1 4.2 collective-permute-done.137
  593.2 4.2 collective-permute-done.143
  597.9 26.2 %all-gather = f32[32,2,4,16]{3,2,1,0:T(4,128)S(1)} all-gather(f32[2,2,4,16]{3,2,1,0:T(4,128)S(1)} %pad_maximum_fusion.737), channel_id=2, replica_groups=mesh['gx'=2,'gy'=4,'gz'=4] {'gy','gz'}, dimensions={0}, use_global_device_ids=true | all-gather | bytes 17408 | tf_op jit(solution)/shard_map/all_gather | solution.py:134
  676.6 4.4 all_gather.7
  743.2 5.8 collective-permute-start.174
  750.7 4.2 collective-permute-done.175
  777.0 4.2 collective-permute-done.181
  803.4 4.2 collective-permute-done.187
  827.8 4.2 collective-permute-done.193
  852.1 4.2 collective-permute-done.199
  876.5 4.2 collective-permute-done.205
  900.7 4.4 collective-permute-done.211
  923.8 4.4 collective-permute-done.217
  946.8 4.4 collective-permute-done.223
  970.1 4.4 collective-permute-done.229
  993.2 4.4 collective-permute-done.235
  1016.3 4.4 collective-permute-done.241
  1026.7 4.2 collective-permute-done.243
  1041.3 5.3 collective-permute-done.246
  1054.2 4.2 collective-permute-done.249
  1069.1 5.3 collective-permute-done.252
  1096.9 5.3 collective-permute-done.258
  1124.8 5.3 collective-permute-done.264
  1152.6 5.3 collective-permute-done.270
  1180.4 5.3 collective-permute-done.276
  (905 shorter events, 844.7 us)
Async XLA Ops:
  0.8 11.7 collective-permute-start.2
  2.1 16.2 %collective-permute-start.1 = (f32[1,32,128]{2,1,0:T(8,128)S(1)}, f32[1,32,128]{2,1,0:T(8,128)S(1)}, u32[]{:S(2)}, u32[]{:S(2)}) collective-permute-start(f32[1,32,128]{2,1,0:T(8,128)S(1)} %broadcast.184), channel_id=1, source_target_pairs={{16,0},{17,1},{18,2},{19,3},{20,4},{21,5},{22,6},{23,7},{24,8},{25... | collective-permute-start | bytes 49160 | tf_op jit(solution)/shard_map/ppermute | solution.py:21
  6.6 11.6 collective-permute-start.3
  13.9 9.5 collective-permute-start.4
  18.4 11.2 collective-permute-start.5
  23.7 13.3 %collective-permute-start.10 = (f32[18,34,1]{2,1,0:T(8,128)S(1)}, f32[18,34,1]{2,1,0:T(8,128)S(1)}, u32[]{:S(2)}, u32[]{:S(2)}) collective-permute-start(f32[18,34,1]{2,1,0:T(8,128)S(1)} %get-tuple-element.206), channel_id=1, source_target_pairs={{0,1},{1,2},{2,3},{4,5},{5,6},{6,7},{8,9},{9,10},{10,11},{12,13},{... | collective-permute-start | bytes 7352 | tf_op jit(solution)/shard_map/ppermute | solution.py:20
  25.0 13.2 %collective-permute-start.8 = (f32[18,34,1]{2,1,0:T(8,128)S(1)}, f32[18,34,1]{2,1,0:T(8,128)S(1)}, u32[]{:S(2)}, u32[]{:S(2)}) collective-permute-start(f32[18,34,1]{2,1,0:T(8,128)S(1)} %get-tuple-element.207), channel_id=1, source_target_pairs={{1,0},{2,1},{3,2},{5,4},{6,5},{7,6},{9,8},{10,9},{11,10},{13,12},{... | collective-permute-start | bytes 7352 | tf_op jit(solution)/shard_map/ppermute | solution.py:21
  29.8 12.8 %collective-permute-start.11 = (f32[18,34,1]{2,1,0:T(8,128)S(1)}, f32[18,34,1]{2,1,0:T(8,128)S(1)}, u32[]{:S(2)}, u32[]{:S(2)}) collective-permute-start(f32[18,34,1]{2,1,0:T(8,128)S(1)} %get-tuple-element.209), channel_id=1, source_target_pairs={{0,1},{1,2},{2,3},{4,5},{5,6},{6,7},{8,9},{9,10},{10,11},{12,13},{... | collective-permute-start | bytes 7352 | tf_op jit(solution)/shard_map/ppermute | solution.py:20
  31.1 12.7 %collective-permute-start.9 = (f32[18,34,1]{2,1,0:T(8,128)S(1)}, f32[18,34,1]{2,1,0:T(8,128)S(1)}, u32[]{:S(2)}, u32[]{:S(2)}) collective-permute-start(f32[18,34,1]{2,1,0:T(8,128)S(1)} %get-tuple-element.208), channel_id=1, source_target_pairs={{1,0},{2,1},{3,2},{5,4},{6,5},{7,6},{9,8},{10,9},{11,10},{13,12},{... | collective-permute-start | bytes 7352 | tf_op jit(solution)/shard_map/ppermute | solution.py:21
  64.1 10.2 collective-permute-start.16
  68.2 10.2 collective-permute-start.17
  95.0 8.8 collective-permute-start.22
  97.4 10.5 collective-permute-start.23
  123.0 8.8 collective-permute-start.28
  125.4 10.5 collective-permute-start.29
  136.4 33.9 %collective-permute-start.30 = (f32[1,32,128]{2,1,0:T(8,128)S(1)}, f32[1,32,128]{2,1,0:T(8,128)S(1)}, u32[]{:S(2)}, u32[]{:S(2)}) collective-permute-start(f32[1,32,128]{2,1,0:T(8,128)S(1)} %get-tuple-element.255), channel_id=1, source_target_pairs={{16,0},{17,1},{18,2},{19,3},{20,4},{21,5},{22,6},{23,7},{24,8},{25... | collective-permute-start | bytes 49160 | tf_op jit(solution)/shard_map/ppermute | solution.py:21
  138.1 32.3 %collective-permute-start.31 = (f32[1,32,128]{2,1,0:T(8,128)S(1)}, f32[1,32,128]{2,1,0:T(8,128)S(1)}, u32[]{:S(2)}, u32[]{:S(2)}) collective-permute-start(f32[1,32,128]{2,1,0:T(8,128)S(1)} %get-tuple-element.254), channel_id=1, source_target_pairs={{0,16},{1,17},{2,18},{3,19},{4,20},{5,21},{6,22},{7,23},{8,24},{9,... | collective-permute-start | bytes 49160 | tf_op jit(solution)/shard_map/ppermute | solution.py:20
  139.4 65.3 %collective-permute-start.49 = (f32[1,16,64]{2,1,0:T(8,128)S(1)}, f32[1,16,64]{2,1,0:T(8,128)S(1)}, u32[]{:S(2)}, u32[]{:S(2)}) collective-permute-start(f32[1,16,64]{2,1,0:T(8,128)S(1)} %broadcast.188), channel_id=1, source_target_pairs={{16,0},{17,1},{18,2},{19,3},{20,4},{21,5},{22,6},{23,7},{24,8},{25... | collective-permute-start | bytes 12296 | tf_op jit(solution)/shard_map/ppermute | solution.py:21
  143.9 62.7 %collective-permute-start.51 = (f32[1,16,64]{2,1,0:T(8,128)S(1)}, f32[1,16,64]{2,1,0:T(8,128)S(1)}, u32[]{:S(2)}, u32[]{:S(2)}) collective-permute-start(f32[1,16,64]{2,1,0:T(8,128)S(1)} %broadcast.188), channel_id=1, source_target_pairs={{0,16},{1,17},{2,18},{3,19},{4,20},{5,21},{6,22},{7,23},{8,24},{9,... | collective-permute-start | bytes 12296 | tf_op jit(solution)/shard_map/ppermute | solution.py:20
  177.7 8.6 collective-permute-start.34
  179.9 10.5 collective-permute-start.35
  181.2 14.2 %collective-permute-start.48 = (f32[1,16,64]{2,1,0:T(8,128)S(1)}, f32[1,16,64]{2,1,0:T(8,128)S(1)}, u32[]{:S(2)}, u32[]{:S(2)}) collective-permute-start(f32[1,16,64]{2,1,0:T(8,128)S(1)} %get-tuple-element.352), channel_id=1, source_target_pairs={{16,0},{17,1},{18,2},{19,3},{20,4},{21,5},{22,6},{23,7},{24,8},{25... | collective-permute-start | bytes 12296 | tf_op jit(solution)/shard_map/ppermute | solution.py:21
  186.3 10.5 collective-permute-start.50
  190.9 8.2 collective-permute-start.36
  196.8 17.9 %collective-permute-start.52 = (f32[10,1,64]{2,1,0:T(1,128)S(1)}, f32[10,1,64]{2,1,0:T(1,128)S(1)}, u32[]{:S(2)}, u32[]{:S(2)}) collective-permute-start(f32[10,1,64]{2,1,0:T(1,128)S(1)} %get-tuple-element.322), channel_id=1, source_target_pairs={{4,0},{8,4},{12,8},{5,1},{9,5},{13,9},{6,2},{10,6},{14,10},{7,3},{... | collective-permute-start | bytes 7688 | tf_op jit(solution)/shard_map/ppermute | solution.py:21
  199.1 16.9 %collective-permute-start.54 = (f32[10,1,64]{2,1,0:T(1,128)S(1)}, f32[10,1,64]{2,1,0:T(1,128)S(1)}, u32[]{:S(2)}, u32[]{:S(2)}) collective-permute-start(f32[10,1,64]{2,1,0:T(1,128)S(1)} %get-tuple-element.321), channel_id=1, source_target_pairs={{0,4},{4,8},{8,12},{1,5},{5,9},{9,13},{2,6},{6,10},{10,14},{3,7},{... | collective-permute-start | bytes 7688 | tf_op jit(solution)/shard_map/ppermute | solution.py:20
  201.2 9.1 collective-permute-start.38
  206.7 33.2 %collective-permute-start.53 = (f32[10,1,64]{2,1,0:T(1,128)S(1)}, f32[10,1,64]{2,1,0:T(1,128)S(1)}, u32[]{:S(2)}, u32[]{:S(2)}) collective-permute-start(f32[10,1,64]{2,1,0:T(1,128)S(1)} %get-tuple-element.324), channel_id=1, source_target_pairs={{4,0},{8,4},{12,8},{5,1},{9,5},{13,9},{6,2},{10,6},{14,10},{7,3},{... | collective-permute-start | bytes 7688 | tf_op jit(solution)/shard_map/ppermute | solution.py:21
  210.3 31.5 %collective-permute-start.55 = (f32[10,1,64]{2,1,0:T(1,128)S(1)}, f32[10,1,64]{2,1,0:T(1,128)S(1)}, u32[]{:S(2)}, u32[]{:S(2)}) collective-permute-start(f32[10,1,64]{2,1,0:T(1,128)S(1)} %get-tuple-element.323), channel_id=1, source_target_pairs={{0,4},{4,8},{8,12},{1,5},{5,9},{9,13},{2,6},{6,10},{10,14},{3,7},{... | collective-permute-start | bytes 7688 | tf_op jit(solution)/shard_map/ppermute | solution.py:20
  212.5 8.3 collective-permute-start.40
  214.7 10.3 collective-permute-start.41
  225.5 8.8 collective-permute-start.42
  231.9 54.6 %collective-permute-start.56 = (f32[10,18,1]{2,1,0:T(8,128)}, f32[10,18,1]{2,1,0:T(8,128)S(1)}, u32[]{:S(2)}, u32[]{:S(2)}) collective-permute-start(f32[10,18,1]{2,1,0:T(8,128)} %get-tuple-element.294), channel_id=1, source_target_pairs={{1,0},{2,1},{3,2},{5,4},{6,5},{7,6},{9,8},{10,9},{11,10},{13,12},{... | collective-permute-start | bytes 2168 | tf_op jit(solution)/shard_map/ppermute | solution.py:21
  234.3 52.2 %collective-permute-start.58 = (f32[10,18,1]{2,1,0:T(8,128)}, f32[10,18,1]{2,1,0:T(8,128)S(1)}, u32[]{:S(2)}, u32[]{:S(2)}) collective-permute-start(f32[10,18,1]{2,1,0:T(8,128)} %get-tuple-element.293), channel_id=1, source_target_pairs={{0,1},{1,2},{2,3},{4,5},{5,6},{6,7},{8,9},{9,10},{10,11},{12,13},{... | collective-permute-start | bytes 2168 | tf_op jit(solution)/shard_map/ppermute | solution.py:20
  245.1 11.7 collective-permute-start.46
  249.4 11.5 collective-permute-start.47
  251.7 34.8 %collective-permute-start.57 = (f32[10,18,1]{2,1,0:T(8,128)}, f32[10,18,1]{2,1,0:T(8,128)S(1)}, u32[]{:S(2)}, u32[]{:S(2)}) collective-permute-start(f32[10,18,1]{2,1,0:T(8,128)} %get-tuple-element.295), channel_id=1, source_target_pairs={{1,0},{2,1},{3,2},{5,4},{6,5},{7,6},{9,8},{10,9},{11,10},{13,12},{... | collective-permute-start | bytes 2168 | tf_op jit(solution)/shard_map/ppermute | solution.py:21
  256.8 30.3 %collective-permute-start.59 = (f32[10,18,1]{2,1,0:T(8,128)}, f32[10,18,1]{2,1,0:T(8,128)}, u32[]{:S(2)}, u32[]{:S(2)}) collective-permute-start(f32[10,18,1]{2,1,0:T(8,128)} %get-tuple-element.296), channel_id=1, source_target_pairs={{0,1},{1,2},{2,3},{4,5},{5,6},{6,7},{8,9},{9,10},{10,11},{12,13},{... | collective-permute-start | bytes 2168 | tf_op jit(solution)/shard_map/ppermute | solution.py:20
  298.2 12.7 %collective-permute-start.62 = (f32[10,1,64]{2,1,0:T(1,128)S(1)}, f32[10,1,64]{2,1,0:T(1,128)S(1)}, u32[]{:S(2)}, u32[]{:S(2)}) collective-permute-start(f32[10,1,64]{2,1,0:T(1,128)S(1)} %get-tuple-element.320), channel_id=1, source_target_pairs={{4,0},{8,4},{12,8},{5,1},{9,5},{13,9},{6,2},{10,6},{14,10},{7,3},{... | collective-permute-start | bytes 7688 | tf_op jit(solution)/shard_map/ppermute | solution.py:21
  300.1 10.8 collective-permute-start.63
  302.6 52.0 %collective-permute-start.97 = (f32[1,8,32]{2,1,0:T(8,128)S(1)}, f32[1,8,32]{2,1,0:T(8,128)S(1)}, u32[]{:S(2)}, u32[]{:S(2)}) collective-permute-start(f32[1,8,32]{2,1,0:T(8,128)S(1)} %broadcast.193), channel_id=1, source_target_pairs={{16,0},{17,1},{18,2},{19,3},{20,4},{21,5},{22,6},{23,7},{24,8},{25... | collective-permute-start | bytes 3080 | tf_op jit(solution)/shard_map/ppermute | solution.py:21
  304.2 51.6 %collective-permute-start.99 = (f32[1,8,32]{2,1,0:T(8,128)S(1)}, f32[1,8,32]{2,1,0:T(8,128)S(1)}, u32[]{:S(2)}, u32[]{:S(2)}) collective-permute-start(f32[1,8,32]{2,1,0:T(8,128)S(1)} %broadcast.193), channel_id=1, source_target_pairs={{0,16},{1,17},{2,18},{3,19},{4,20},{5,21},{6,22},{7,23},{8,24},{9,... | collective-permute-start | bytes 3080 | tf_op jit(solution)/shard_map/ppermute | solution.py:20
  320.2 10.4 collective-permute-start.66
  344.2 30.5 %collective-permute-start.102 = (f32[6,1,32]{2,1,0:T(1,128)S(1)}, f32[6,1,32]{2,1,0:T(1,128)S(1)}, u32[]{:S(2)}, u32[]{:S(2)}) collective-permute-start(f32[6,1,32]{2,1,0:T(1,128)S(1)} %get-tuple-element.434), channel_id=1, source_target_pairs={{0,4},{4,8},{8,12},{1,5},{5,9},{9,13},{2,6},{6,10},{10,14},{3,7},{... | collective-permute-start | bytes 2312 | tf_op jit(solution)/shard_map/ppermute | solution.py:20
  346.1 47.1 %collective-permute-start.100 = (f32[6,1,32]{2,1,0:T(1,128)S(1)}, f32[6,1,32]{2,1,0:T(1,128)S(1)}, u32[]{:S(2)}, u32[]{:S(2)}) collective-permute-start(f32[6,1,32]{2,1,0:T(1,128)S(1)} %get-tuple-element.433), channel_id=1, source_target_pairs={{4,0},{8,4},{12,8},{5,1},{9,5},{13,9},{6,2},{10,6},{14,10},{7,3},{... | collective-permute-start | bytes 2312 | tf_op jit(solution)/shard_map/ppermute | solution.py:21
  364.4 43.4 %collective-permute-start.103 = (f32[6,1,32]{2,1,0:T(1,128)S(1)}, f32[6,1,32]{2,1,0:T(1,128)S(1)}, u32[]{:S(2)}, u32[]{:S(2)}) collective-permute-start(f32[6,1,32]{2,1,0:T(1,128)S(1)} %get-tuple-element.436), channel_id=1, source_target_pairs={{0,4},{4,8},{8,12},{1,5},{5,9},{9,13},{2,6},{6,10},{10,14},{3,7},{... | collective-permute-start | bytes 2312 | tf_op jit(solution)/shard_map/ppermute | solution.py:20
  366.4 59.9 %collective-permute-start.101 = (f32[6,1,32]{2,1,0:T(1,128)S(1)}, f32[6,1,32]{2,1,0:T(1,128)S(1)}, u32[]{:S(2)}, u32[]{:S(2)}) collective-permute-start(f32[6,1,32]{2,1,0:T(1,128)S(1)} %get-tuple-element.435), channel_id=1, source_target_pairs={{4,0},{8,4},{12,8},{5,1},{9,5},{13,9},{6,2},{10,6},{14,10},{7,3},{... | collective-permute-start | bytes 2312 | tf_op jit(solution)/shard_map/ppermute | solution.py:21
  395.9 8.8 collective-permute-start.82
  400.1 40.9 %collective-permute-start.104 = (f32[6,10,1]{2,0,1:T(8,128)S(1)}, f32[6,10,1]{2,0,1:T(8,128)S(1)}, u32[]{:S(2)}, u32[]{:S(2)}) collective-permute-start(f32[6,10,1]{2,0,1:T(8,128)S(1)} %get-tuple-element.404), channel_id=1, source_target_pairs={{1,0},{2,1},{3,2},{5,4},{6,5},{7,6},{9,8},{10,9},{11,10},{13,12},{... | collective-permute-start | bytes 728 | tf_op jit(solution)/shard_map/ppermute | solution.py:21
  404.7 38.8 %collective-permute-start.106 = (f32[6,10,1]{2,0,1:T(8,128)S(1)}, f32[6,10,1]{2,0,1:T(8,128)S(1)}, u32[]{:S(2)}, u32[]{:S(2)}) collective-permute-start(f32[6,10,1]{2,0,1:T(8,128)S(1)} %get-tuple-element.403), channel_id=1, source_target_pairs={{0,1},{1,2},{2,3},{4,5},{5,6},{6,7},{8,9},{9,10},{10,11},{12,13},{... | collective-permute-start | bytes 728 | tf_op jit(solution)/shard_map/ppermute | solution.py:20
  434.9 16.1 %collective-permute-start.105 = (f32[6,10,1]{2,0,1:T(8,128)S(1)}, f32[6,10,1]{2,0,1:T(8,128)S(1)}, u32[]{:S(2)}, u32[]{:S(2)}) collective-permute-start(f32[6,10,1]{2,0,1:T(8,128)S(1)} %get-tuple-element.407), channel_id=1, source_target_pairs={{1,0},{2,1},{3,2},{5,4},{6,5},{7,6},{9,8},{10,9},{11,10},{13,12},{... | collective-permute-start | bytes 728 | tf_op jit(solution)/shard_map/ppermute | solution.py:21
  436.8 14.2 %collective-permute-start.107 = (f32[6,10,1]{2,0,1:T(8,128)S(1)}, f32[6,10,1]{2,0,1:T(8,128)S(1)}, u32[]{:S(2)}, u32[]{:S(2)}) collective-permute-start(f32[6,10,1]{2,0,1:T(8,128)S(1)} %get-tuple-element.408), channel_id=1, source_target_pairs={{0,1},{1,2},{2,3},{4,5},{5,6},{6,7},{8,9},{9,10},{10,11},{12,13},{... | collective-permute-start | bytes 728 | tf_op jit(solution)/shard_map/ppermute | solution.py:20
  1038.0 8.5 collective-permute-start.246
  1040.0 10.7 collective-permute-start.247
  1065.6 8.8 collective-permute-start.252
  1067.8 10.7 collective-permute-start.253
  1093.4 8.8 collective-permute-start.258
  1095.6 10.7 collective-permute-start.259
  1121.2 8.8 collective-permute-start.264
  1123.5 10.7 collective-permute-start.265
  1149.1 8.8 collective-permute-start.270
  1151.3 10.7 collective-permute-start.271
  1176.9 8.8 collective-permute-start.276
  1179.1 10.7 collective-permute-start.277
  (218 other events, 1322.9 us)
where the time goes:
time: 1210 us; the launch traced here: 1190 us
  starting transfers between devices  573 us (47%)
  waiting for transfers between devices  467 us (39%)
  local copies, waits for them, and re-layouts  72.8 us (6%)
  other arithmetic  43.3 us (4%)
  blocking collectives  30.6 us (3%)
    ppermute x139, waiting for transfers between devices, with_halo(): before = lax.ppermute(last, axis, up)  387 us
    ppermute x139, starting transfers between devices, with_halo(): after = lax.ppermute(first, axis, down)  356 us
    ppermute x139, starting transfers between devices, with_halo(): before = lax.ppermute(last, axis, up)  217 us
    ppermute x139, waiting for transfers between devices, with_halo(): after = lax.ppermute(first, axis, down)  80.4 us
    reshape x4, local copies, waits for them, and re-layouts, restrict(): blocks = field.reshape(shape[0] // 2, 2, shape[1] // 2, 2, shape[2] // 2, 2)  40 us
    all_gather x1, blocking collectives, shards(): gathered = lax.all_gather(stacked, ('gy', 'gz'), axis=0, tiled=True)  26.2 us
  transfers between devices with their start and end apart: 278, of which 160 were waited for; matrix products, arithmetic and copies ran while one was open for 6% of the time, Pallas kernels for 0%

commit v1 on v0

--- a/solution.py
+++ b/solution.py
@@ -1,13 +1,16 @@
+import functools
+
 import jax
 import jax.numpy as jnp
 from jax import lax
+from jax.experimental import pallas as pl
+from jax.experimental.pallas import tpu as pltpu
 from jax.sharding import PartitionSpec as P
 
 SWEEPS = 6
 COARSE_SWEEPS = 16
-
-
 DAMPING = 0.8
+VMEM_BYTES = 32 * 2**20
 
 
 def with_halo(array, sides, width):
@@ -113,7 +116,7 @@
     return field
 
 
-def shards(source, conductivity):
+def plain_shards(source, conductivity):
     count_x, count_y, count_z = (lax.axis_size("gx"), lax.axis_size("gy"), lax.axis_size("gz"))
     place_x, place_y, place_z = (lax.axis_index("gx"), lax.axis_index("gy"), lax.axis_index("gz"))
     rhs_level = source
@@ -151,7 +154,679 @@
     return result
 
 
+ROWS = 48
+MARGIN = 8
+MAIN = MARGIN + 25 * ROWS + MARGIN
+STRIP = MARGIN + 5 * ROWS + MARGIN
+SECOND = MARGIN + 18 * ROWS + MARGIN
+
+
+def roll(value, shift, axis):
+    if isinstance(shift, int):
+        shift = shift % value.shape[axis]
+        if shift == 0:
+            return value
+    return pltpu.roll(value, shift, axis)
+
+
+def iota(shape, axis):
+    return lax.broadcasted_iota(jnp.int32, shape, axis)
+
+
+def gather_lanes(value, lanes):
+    return jnp.take_along_axis(value, lanes, axis=1, mode="promise_in_bounds")
+
+
+def block(at, count):
+    return pl.ds(pl.multiple_of(at, 8) if not isinstance(at, int) else at, count)
+
+
+def terms(coef, nears, rhs, weight):
+    faces = [0.5 * (coef + near) for near in nears]
+    total = functools.reduce(lambda a, b: a + b, faces)
+    scale = jnp.where(coef > 0.0, DAMPING / total, 0.0)
+    return faces, scale, rhs * scale * (1.0 / weight), total * (weight / DAMPING)
+
+
+def each(count, body, step):
+    def several(turn, carry):
+        for ahead in range(step):
+            body(turn * step + ahead)
+        return carry
+
+    def single(index, carry):
+        body(index)
+        return carry
+
+    whole = count // step
+    lax.fori_loop(0, whole, several, 0)
+    if count % step:
+        lax.fori_loop(whole * step, count, single, 0)
+
+
+def row_pairs(array, rows):
+    return array[pl.ds(0, rows // 2, stride=2), :] + array[pl.ds(1, rows // 2, stride=2), :]
+
+
+def repeat_rows(array, value):
+    rows = value.shape[0]
+    array[pl.ds(0, rows, stride=2), :] = value
+    array[pl.ds(1, rows, stride=2), :] = value
+
+
+def lane_pairs(value):
+    return value + roll(value, -1, 1)
+
+
+def both_ways(face, value, axis):
+    return face * roll(value, -1, axis) + roll(face * value, 1, axis)
+
+
+def by_side(swapped, odd):
+    first, second = swapped
+    return jnp.where(odd, first, second), jnp.where(odd, second, first)
+
+
+def device_place():
+    return [lax.axis_index(axis) for axis in ("gx", "gy", "gz")]
+
+
+def odd_at(place, axis):
+    return (place[axis] & 1) == 1
+
+
+def with_tiles(middle, first, second, odd):
+    sides = [by_side(tiles, odd) for tiles in zip(first, second)]
+    return jnp.concatenate([low for low, _ in sides] + list(middle) + [high for _, high in sides], axis=0)
+
+
+def main_at(plane):
+    return MARGIN + ROWS * plane
+
+
+def joined(middle, edge):
+    lane = iota(middle.shape, 1)
+    return jnp.where(lane == 127, edge, roll(middle, -1, 1)), jnp.where(lane == 0, edge, roll(middle, 1, 1))
+
+
+def facing(own, plane, slot):
+    lane = iota(own.shape, 1)
+    return jnp.where((lane == 16 * slot + 7) | (lane == 16 * slot + 8), roll(plane, 16 * slot + 8, 1), own)
+
+
+def strip_nears(strip, own, group):
+    at = main_at(group + 1)
+    middle = strip[block(at, ROWS)]
+    lane = iota((ROWS, 128), 1)
+    slot_lane = lane & 15
+    further = jnp.where(lane < 112, roll(middle, -16, 1), roll(strip[block(at + ROWS, ROWS)], -16, 1))
+    nearer = jnp.where(lane >= 16, roll(middle, 16, 1), roll(strip[block(at - ROWS, ROWS)], 16, 1))
+    after = jnp.where(slot_lane == 7, own, roll(middle, -1, 1))
+    before = jnp.where(slot_lane == 8, own, roll(middle, 1, 1))
+    return middle, [further, nearer, roll(middle, -1, 0), roll(middle, 1, 0), after, before]
+
+
+def finest_terms(rhs, coef, kept, inverse):
+    main, strip = coef
+
+    def group(index, slots):
+        first = 8 * index + 1
+        before = main[block(main_at(first - 1), ROWS)]
+        here = main[block(main_at(first), ROWS)]
+        held = strip[block(main_at(index + 1), ROWS)]
+        own = jnp.zeros((ROWS, 128), jnp.float32)
+        for slot in range(slots):
+            at = block(main_at(first + slot), ROWS)
+            after = main[block(main_at(first + slot + 1), ROWS)]
+            nears = [after, before, roll(here, -1, 0), roll(here, 1, 0), *joined(here, roll(held, 120 - 16 * slot, 1))]
+            faces, scale, start, back = terms(here, nears, rhs[0][at], 1.0)
+            for side, value in enumerate((faces[0], faces[2], faces[4], faces[5], scale, start)):
+                kept[0][side, at] = value
+            inverse[at] = back
+            own = facing(own, here, slot)
+            before, here = here, after
+        for slot in range(slots, 8):
+            own = facing(own, main[block(main_at(first + slot), ROWS)], slot)
+        at = block(main_at(index + 1), ROWS)
+        middle, nears = strip_nears(strip, own, index)
+        faces, scale, start, _ = terms(middle, nears, rhs[1][at], 1.0)
+        for side in range(6):
+            kept[1][side, at] = faces[side] * scale
+        kept[1][6, at] = start
+
+    each(2, lambda index: group(index, 8), 1)
+    group(2, 6)
+
+
+def finest_sweep(count, kept, source, target, keep=1.0 - DAMPING, strips=True):
+    main, strip = source
+
+    def group(index, slots):
+        first = 8 * index + 1
+        at = block(main_at(first - 1), ROWS)
+        flux = kept[0][0, at] * main[at]
+        here = main[block(main_at(first), ROWS)]
+        held = strip[block(main_at(index + 1), ROWS)]
+        own = jnp.zeros((ROWS, 128), jnp.float32)
+        for slot in range(slots):
+            at = block(main_at(first + slot), ROWS)
+            after = main[block(main_at(first + slot + 1), ROWS)]
+            face = kept[0][0, at]
+            total = flux + face * after
+            flux = face * here
+            total = total + both_ways(kept[0][1, at], here, 0)
+            above, below = joined(here, roll(held, 120 - 16 * slot, 1))
+            total = total + kept[0][2, at] * above + kept[0][3, at] * below
+            target[0][at] = kept[0][5, at] + keep * here + kept[0][4, at] * total
+            if strips:
+                own = facing(own, here, slot)
+            here = after
+        if strips:
+            at = block(main_at(index + 1), ROWS)
+            middle, nears = strip_nears(strip, own, index)
+            total = kept[1][6, at] + keep * middle
+            for side, near in enumerate(nears):
+                total = total + kept[1][side, at] * near
+            target[1][at] = total
+
+    each(2, lambda index: group(index, 8), 1)
+    if count > 16:
+        group(2, count - 16)
+
+
+def strip_pages(rhs_planes, coef_planes):
+    lane = iota((32, 128), 1)
+    left = jnp.zeros((32, 128), jnp.float32)
+    right = jnp.zeros((32, 128), jnp.float32)
+    for field_at, planes in ((0, rhs_planes), (8, coef_planes)):
+        for slot, plane in enumerate(planes):
+            at = 16 * slot + field_at
+            inside = (lane >= at) & (lane < at + 8)
+            left = jnp.where(inside, gather_lanes(plane, 7 - (lane & 7)), left)
+            right = jnp.where(inside, gather_lanes(plane, 127 - (lane & 7)), right)
+    return left, right
+
+
+def plane_kernel(rhs, coef, fields, message):
+    side = lax.axis_index("gx")
+    for field_at, array in enumerate((rhs, coef)):
+        for local in range(16):
+            plane = array[local + side * (15 - 2 * local)]
+            fields[16 * field_at + local] = plane
+            if local > 9 - field_at:
+                message[6 * field_at + 15 - local] = plane
+
+
+def edge_kernel(fields, to_first, to_second, rows_first, rows_second):
+    place = device_place()
+    odd, odd_y = odd_at(place, 2), odd_at(place, 1)
+    for group in range(2):
+        planes = [[fields[16 * field_at + 8 * group + slot] for slot in range(8)] for field_at in range(2)]
+        to_first[group], to_second[group] = by_side(strip_pages(*planes), odd)
+    for page in range(32):
+        rows_first[page], rows_second[page] = by_side((fields[page, 0:8], fields[page, 24:32]), odd_y)
+
+
+def mirrored_slots(value):
+    lane = iota(value.shape, 1)
+    found = value
+    for slot in range(8):
+        inside = (lane >= 16 * slot) & (lane < 16 * slot + 16)
+        found = jnp.where(inside, roll(value, 16 * (2 * slot - 7), 1), found)
+    return found
+
+
+def finest_kernel(own, strips, own_first, own_second, strip_first, strip_second, partner, beside, corner, pre, lower, message,
+                  to_first, to_second, kept, kept_strip, rhs, rhs_strip, coef, coef_strip, va, va_strip, vb, vb_strip, inverse,
+                  sums):
+    place = device_place()
+    blank = jnp.zeros((ROWS, 128), jnp.float32)
+    outside = block(main_at(0), ROWS)
+    for array in (coef, va, vb):
+        array[outside] = blank
+    coef[block(main_at(24), ROWS)] = blank
+    kept[0, outside] = blank
+    kept[5, outside] = blank
+    for array in (coef_strip, va_strip, vb_strip, kept_strip.at[6]):
+        array[outside] = blank
+        array[block(main_at(4), ROWS)] = blank
+    odd_y, odd_z = odd_at(place, 1), odd_at(place, 2)
+
+    no_rows = jnp.zeros((8, 128), jnp.float32)
+    for local in range(23):
+        at = block(main_at(local + 1), ROWS)
+        for field_at, array in enumerate((rhs, coef)):
+            if local < 16:
+                page = 16 * field_at + local
+                array[at] = with_tiles([own[page]], [own_first[page]], [own_second[page]], odd_y)
+            elif local < 22 + field_at:
+                step = local - 16
+                page = 12 + 6 * field_at - step
+                beyond = step == 5 + field_at
+                first, second = (no_rows, no_rows) if beyond else (beside[page], beside[11 + page])
+                array[at] = with_tiles([partner[6 * field_at + step]], [first], [second], odd_y)
+    above = (iota((ROWS, 128), 1) & 15) < 8
+    for group in range(3):
+        pages = []
+        for which in range(2):
+            if group < 2:
+                page = 2 - 2 * which + group
+                pages.append(with_tiles([strips[page]], [strip_first[page]], [strip_second[page]], odd_y))
+            else:
+                tiles = [beside[4 - 4 * which + part] for part in range(4)]
+                pages.append(with_tiles(tiles, [corner[1 - which]], [corner[3 - which]], odd_y))
+        left, right = by_side(pages, odd_z)
+        if group == 2:
+            left, right = mirrored_slots(left), mirrored_slots(right)
+        at = block(main_at(group + 1), ROWS)
+        rhs_strip[at] = jnp.where(above, right, roll(left, 8, 1))
+        coef_strip[at] = jnp.where(above, roll(right, -8, 1), left)
+    both = (kept, kept_strip)
+    finest_terms((rhs, rhs_strip), (coef, coef_strip), both, inverse)
+    a, b = (va, va_strip), (vb, vb_strip)
+    source = (kept.at[5], kept_strip.at[6])
+    for count, target in zip(range(21, 16, -1), (a, b, a, b, a)):
+        finest_sweep(count, both, source, target)
+        source = target
+    finest_sweep(16, both, a, b, -DAMPING, False)
+
+    def pair(index):
+        total = jnp.zeros((32, 128), jnp.float32)
+        conduct = jnp.zeros((32, 128), jnp.float32)
+        for local in (2 * index, 2 * index + 1):
+            at = block(main_at(local + 1) + 8, 32)
+            value = va[at]
+            pre[local] = value
+            total = total + vb[at] * inverse[at]
+            conduct = conduct + coef[at]
+        sums[block(index * 32, 32)] = total
+        sums[block(index * 32 + 256, 32)] = conduct
+
+    each(8, pair, 4)
+    folded = lane_pairs(row_pairs(sums, 512)) * 0.125
+    lane = iota((128, 128), 1)
+    merged = jnp.where(lane < 64, gather_lanes(folded[0:128], (2 * lane) & 127), gather_lanes(folded[128:256], (2 * lane) & 127))
+    lane = iota((16, 128), 1)
+    for group in range(2):
+        right = jnp.zeros((16, 128), jnp.float32)
+        left = jnp.zeros((16, 128), jnp.float32)
+        for slot in range(4):
+            local = 4 * group + slot
+            plane = merged[16 * local : 16 * local + 16]
+            lower[local] = plane
+            message[2 * local] = plane[0:8]
+            message[2 * local + 1] = plane[8:16]
+            for field_at in range(2):
+                at = 32 * slot + 16 * field_at
+                inside = (lane >= at) & (lane < at + 16)
+                right = jnp.where(inside, roll(plane, at - 48 - 64 * field_at, 1), right)
+                left = jnp.where(inside, roll(plane, at - 64 * field_at, 1), left)
+        rows = slice(16 * group, 16 * group + 16)
+        to_first[rows], to_second[rows] = by_side((left, right), odd_z)
+    lane = iota((32, 128), 1)
+    mirrored = jnp.where((lane & 15) < 8, 7 - (lane & 15), 135 - (lane & 15))
+    for local in range(10, 16):
+        for part in range(4):
+            message[4 * local - 24 + part] = pre[local, 8 * part : 8 * part + 8]
+    for group in range(2):
+        value = jnp.zeros((32, 128), jnp.float32)
+        for slot in range(8):
+            inside = (lane >= 16 * slot) & (lane < 16 * slot + 16)
+            value = jnp.where(inside, gather_lanes(pre[8 * group + slot], mirrored), value)
+        rows = slice(64 - 32 * group, 96 - 32 * group)
+        to_first[rows] = value
+        to_second[rows] = value
+
+
+def second_window(place, own, first, second, rhs, coef):
+    lane = iota((ROWS, 128), 1)
+    odd_y, odd_z = odd_at(place, 1), odd_at(place, 2)
+
+    def page(index):
+        low, high = by_side((first[2 * index], second[2 * index]), odd_y)
+        low_next, high_next = by_side((first[2 * index + 1], second[2 * index + 1]), odd_y)
+        return jnp.concatenate([low, low_next, own[index], high, high_next], axis=0)
+
+    for group in range(4):
+        at = (8 + group) if group < 2 else 18 + group
+        left, right = by_side((page(at), page(at + 2)), odd_z)
+        for slot in range(4):
+            other = 4 * group + slot
+            local, middle = (other, page(other)) if group < 2 else (23 - other, page(4 + other))
+            for field_at, array in enumerate((rhs, coef)):
+                at = 32 * slot + 16 * field_at
+                value = jnp.where(lane < 64, roll(middle, -64 * field_at, 1), 0.0)
+                value = jnp.where((lane >= 64) & (lane < 80), roll(right, 64 - at, 1), value)
+                array[block(main_at(local + 1), ROWS)] = jnp.where(lane >= 112, roll(left, 112 - at, 1), value)
+
+
+def second_sweep(count, kept, source, target, skip=0, keep=1.0 - DAMPING):
+    rows = ROWS - 2 * skip
+    at = block(main_at(0) + skip, rows)
+    flux = kept[0, at] * source[at]
+    here = source[block(main_at(1) + skip, rows)]
+    for plane in range(1, count + 1):
+        at = block(main_at(plane) + skip, rows)
+        after = source[block(main_at(plane + 1) + skip, rows)]
+        face = kept[0, at]
+        total = flux + face * after
+        flux = face * here
+        total = total + both_ways(kept[1, at], here, 0) + both_ways(kept[2, at], here, 1)
+        target[at] = kept[4, at] + keep * here + kept[3, at] * total
+        here = after
+
+
+def second_kernel(own, first, second, share, va, kept, rhs, coef, inverse, vb, sums):
+    place = device_place()
+    blank = jnp.zeros((ROWS, 128), jnp.float32)
+    for plane in (0, 17):
+        at = block(main_at(plane), ROWS)
+        for array in (coef, va, vb, kept.at[0], kept.at[4]):
+            array[at] = blank
+    second_window(place, own, first, second, rhs, coef)
+
+    def plane(index):
+        at = block(main_at(index + 1), ROWS)
+        here = coef[at]
+        nears = [coef[block(main_at(index + 2), ROWS)], coef[block(main_at(index), ROWS)],
+                 roll(here, -1, 0), roll(here, 1, 0), roll(here, -1, 1), roll(here, 1, 1)]
+        faces, scale, start, inverse[at] = terms(here, nears, rhs[at], 0.25)
+        for side, value in enumerate((faces[0], faces[2], faces[4], scale, start)):
+            kept[side, at] = value
+
+    each(16, plane, 4)
+    second_sweep(16, kept, kept.at[4], va)
+
+    def twice(index, carry):
+        second_sweep(16, kept, va, vb)
+        second_sweep(16, kept, vb, va)
+        return carry
+
+    lax.fori_loop(0, 2, twice, 0)
+    second_sweep(16, kept, va, vb, 8, -DAMPING)
+    for local in range(8):
+        residual = jnp.zeros((16, 128), jnp.float32)
+        conduct = jnp.zeros((16, 128), jnp.float32)
+        for here in (2 * local + 1, 2 * local + 2):
+            at = block(main_at(here) + 16, 16)
+            residual = residual + vb[at] * inverse[at]
+            conduct = conduct + coef[at]
+        sums[16 * local : 16 * local + 16] = residual
+        sums[128 + 16 * local : 144 + 16 * local] = conduct
+    folded = lane_pairs(row_pairs(sums, 256)) * 0.125
+    lane = iota((8, 128), 1)
+    for group in range(4):
+        value = jnp.zeros((8, 128), jnp.float32)
+        for plane in range(2):
+            for field_at in range(2):
+                row = 64 * field_at + 8 * (2 * group + plane)
+                at = 64 * plane + 32 * field_at
+                inside = (lane >= at) & (lane < at + 32)
+                value = jnp.where(inside, gather_lanes(folded[row : row + 8], (2 * lane) & 63), value)
+        for device in range(share.shape[0]):
+            share[device, group] = value
+
+
+def whole_terms(planes, rows, lanes, rhs, coef, kept, weight):
+    row = iota((rows, 128), 0)
+    lane = iota((rows, 128), 1)
+    outside = jnp.zeros((rows, 128), jnp.float32)
+    held = [outside] + [coef[here] for here in range(planes)] + [outside]
+    for here in range(planes):
+        middle = held[here + 1]
+        nears = [
+            held[here + 2], held[here],
+            jnp.where(row == rows - 1, 0.0, roll(middle, -1, 0)), jnp.where(row == 0, 0.0, roll(middle, 1, 0)),
+            jnp.where(lane >= lanes - 1, 0.0, roll(middle, -1, 1)), jnp.where(lane == 0, 0.0, roll(middle, 1, 1))]
+        faces, scale, start, back = terms(middle, nears, rhs[here], weight)
+        for side in range(3):
+            kept[side, here] = jnp.where(nears[2 * side] > 0.0, faces[2 * side], 0.0)
+        kept[3, here] = scale
+        kept[4, here] = start
+        kept[5, here] = back
+
+
+def whole_change(kept, values, keep):
+    found = []
+    flux = None
+    for here, value in enumerate(values):
+        total = both_ways(kept[1, here], value, 0) + both_ways(kept[2, here], value, 1)
+        if here > 0:
+            total = total + flux
+        if here + 1 < len(values):
+            face = kept[0, here]
+            total = total + face * values[here + 1]
+            flux = face * value
+        found.append(kept[4, here] + keep * value + kept[3, here] * total)
+    return tuple(found)
+
+
+def whole_sweeps(count, kept, values):
+    return lax.fori_loop(0, count, lambda index, held: whole_change(kept, held, 1.0 - DAMPING), tuple(values))
+
+
+def whole_solve(level, scratch):
+    kept, rhs, coef, rows_of = scratch[0]
+    planes, rows = rhs.shape[0], rhs.shape[1]
+    lanes = 128 >> (level - 2)
+    whole_terms(planes, rows, lanes, rhs, coef, kept, 0.25**level)
+    start = [kept[4, here] for here in range(planes)]
+    values = whole_sweeps((COARSE_SWEEPS if level == 4 else SWEEPS) - 1, kept, start)
+    if level < 4:
+        residual = [value * kept[5, here] for here, value in enumerate(whole_change(kept, values, -DAMPING))]
+        size = planes // 2 * rows
+        for pair in range(planes // 2):
+            at = pair * rows
+            rows_of[at : at + rows] = residual[2 * pair] + residual[2 * pair + 1]
+            rows_of[size + at : size + at + rows] = coef[2 * pair] + coef[2 * pair + 1]
+        folded = lane_pairs(row_pairs(rows_of, 2 * size)) * 0.125
+        lane = iota(folded.shape, 1)
+        folded = jnp.where(lane < lanes // 2, gather_lanes(folded, (2 * lane) & 127), 0.0)
+        half = rows // 2
+        for pair in range(planes // 2):
+            scratch[1][1][pair] = folded[pair * half : pair * half + half]
+            scratch[1][2][pair] = folded[size // 2 + pair * half : size // 2 + pair * half + half]
+        lower = jnp.concatenate(whole_solve(level + 1, scratch[1:]), axis=0)
+        repeat_rows(rows_of.at[0:size], gather_lanes(lower, lax.shift_right_logical(iota(lower.shape, 1), 1)))
+        values = [
+            value + rows_of[here // 2 * rows : here // 2 * rows + rows] for here, value in enumerate(values)]
+        values = whole_sweeps(SWEEPS, kept, values)
+    return list(values)
+
+
+def whole_scratch(planes, rows):
+    return [field(6, planes, rows, 128), field(planes, rows, 128), field(planes, rows, 128), field(planes * rows, 128)]
+
+
+def third_whole(shares, count_y, count_z, rhs, coef):
+    lane = iota((8, 128), 1)
+    width = 128 // count_z
+    for local in range(8):
+        for at_y in range(count_y):
+            for index, array in enumerate((rhs, coef)):
+                value = jnp.zeros((8, 128), jnp.float32)
+                for at_z in range(count_z):
+                    held = shares[at_y * count_z + at_z, local // 2]
+                    at = 64 * (local % 2) + 32 * index
+                    inside = (lane >= width * at_z) & (lane < width * at_z + width)
+                    value = jnp.where(inside, roll(held, width * at_z - at, 1), value)
+                array[local, 8 * at_y : 8 * at_y + 8] = value
+
+
+def last_kernel(count_y, count_z, own2, first1, second1, shares, pre1, kept1, kept, kept_strip, out, *scratch):
+    place = device_place()
+    deep = [scratch[0:4], scratch[4:8], scratch[8:12]]
+    va1, vb1, va, va_strip, vb, vb_strip = scratch[12:18]
+    framed, twice1, twice0 = scratch[18:21]
+    third_whole(shares, count_y, count_z, deep[0][1], deep[0][2])
+    third = whole_solve(2, deep)
+
+    blank = jnp.zeros((ROWS, 128), jnp.float32)
+    for array, outer in ((va1, 17), (va_strip, 4), (vb_strip, 4)):
+        array[block(main_at(outer), ROWS)] = blank
+    for array in (va1, va, va_strip, vb, vb_strip):
+        array[block(main_at(0), ROWS)] = blank
+    rows = third[0].shape[0]
+    for index, plane in enumerate(third):
+        framed[index, 0:8] = blank[0:8]
+        framed[index, 8 : 8 + rows] = plane
+        framed[index, 8 + rows : 16 + rows] = blank[0:8]
+    for index in range(8):
+        near = framed[index, pl.ds(pl.multiple_of(8 * place[1], 8), 24), :]
+        repeat_rows(twice1.at[48 * index : 48 * index + 48], near)
+    lane = iota((ROWS, 128), 1)
+    held = lax.shift_right_arithmetic(jnp.where(lane < 96, lane, lane - 128), 1) + 32 * place[2]
+    inside = (held >= 0) & (held < 128) & ((lane < 80) | (lane >= 112))
+    for index in range(8):
+        wide = jnp.where(inside, gather_lanes(twice1[48 * index : 48 * index + 48], held & 127), 0.0)
+        for here in (2 * index + 1, 2 * index + 2):
+            there = block(main_at(here), ROWS)
+            va1[there] = pre1[there] + jnp.where(kept1[3, there] > 0.0, wide, 0.0)
+    vb1[block(main_at(0), ROWS)] = blank
+    vb1[block(main_at(17), ROWS)] = blank
+    source, target = va1, vb1
+    for sweep in range(SWEEPS):
+        second_sweep(16 - sweep, kept1, source, target, 8 if sweep else 0)
+        source, target = target, source
+
+    odd_y = odd_at(place, 1)
+
+    def page(index):
+        low, high = by_side((first1[48 + index], second1[48 + index]), odd_y)
+        return jnp.concatenate([low, own2[index], high], axis=0)
+
+    slot_lane = lane & 15
+    above = slot_lane < 8
+    facing_lane = jnp.where(above, 64 + lax.shift_right_logical(7 - slot_lane, 1), 127 - lax.shift_right_logical(slot_lane - 8, 1))
+    for group in range(3):
+        more = jnp.zeros((ROWS, 128), jnp.float32)
+        for index in range(4 * group, min(4 * group + 4, 11)):
+            at = main_at(index + 1) + 8
+            repeat_rows(twice0, source[at : at + 32])
+            near = twice0[8:56]
+            wide = gather_lanes(near, lax.shift_right_logical(lane, 1))
+            at = 32 * (index - 4 * group)
+            more = jnp.where((lane >= at) & (lane < at + 32), gather_lanes(near, facing_lane & 127), more)
+            for local in (2 * index, 2 * index + 1):
+                there = block(main_at(local + 1), ROWS)
+                middle = page(local if local < 16 else 39 - local)
+                va[there] = middle + jnp.where(kept[4, there] > 0.0, wide, 0.0)
+        value = mirrored_slots(page(24)) if group == 2 else page(17 - group)
+        there = block(main_at(group + 1), ROWS)
+        va_strip[there] = value + jnp.where(kept_strip[0, there] > 0.0, more, 0.0)
+    source, target = (va, va_strip), (vb, vb_strip)
+    for count in range(21, 15, -1):
+        finest_sweep(count, (kept, kept_strip), source, target, strips=count > 16)
+        source, target = target, source
+
+    def leave(local):
+        out[local + place[0] * (15 - 2 * local)] = source[0][block(main_at(local + 1) + 8, 32)]
+
+    each(16, leave, 4)
+
+
+def call(kernel, inputs, outs, scratch):
+    near = pl.BlockSpec(memory_space=pltpu.VMEM)
+    return pl.pallas_call(
+        kernel,
+        out_shape=[jax.ShapeDtypeStruct(shape, jnp.float32) for shape in outs],
+        in_specs=[near] * len(inputs),
+        out_specs=[near] * len(outs),
+        scratch_shapes=scratch,
+        compiler_params=pltpu.CompilerParams(vmem_limit_bytes=VMEM_BYTES),
+    )(*inputs)
+
+
+def field(*shape):
+    return pltpu.VMEM(shape, jnp.float32)
+
+
+def from_sides(axis, to_first, to_second):
+    size = lax.axis_size(axis)
+    found = []
+    for message, begin in ((to_second, 1), (to_first, 0)):
+        lower = [(i, i + 1) for i in range(begin, size - 1, 2)]
+        found.append(lax.ppermute(message, axis, lower + [(j, i) for i, j in lower]))
+    return found[::-1]
+
+
+def edge_rows(array, axis, last):
+    odd = lax.axis_index(axis) % 2
+    rows = array.shape[1]
+    return lax.dynamic_slice_in_dim(array, (rows - 8) * (odd if last else 1 - odd), 8, 1)
+
+
+def from_partner(message):
+    return lax.ppermute(message, "gx", [(0, 1), (1, 0)])
+
+
+def merged_sides(first, second):
+    odd = lax.axis_index("gz") % 2 == 1
+    above = lax.broadcasted_iota(jnp.int32, first.shape, first.ndim - 1) % 16 < 8
+    return jnp.where(above == odd, second, first)
+
+
+def fast_shards(source, conductivity):
+    count_y, count_z = lax.axis_size("gy"), lax.axis_size("gz")
+    own, message = call(plane_kernel, (source, conductivity), [(32, 32, 128), (13, 32, 128)], [])
+    to_first, to_second, *rows = call(
+        edge_kernel, (own,), [(2, 32, 128), (2, 32, 128), (32, 8, 128), (32, 8, 128)], [])
+    partner = from_partner(message)
+    strips = jnp.concatenate(from_sides("gz", to_first, to_second)[::-1])
+    own_rev = from_sides("gy", *rows)[::-1]
+    own_rev = lax.optimization_barrier(own_rev)
+    own_rows = own_rev[::-1]
+    strip_rows = from_sides("gy", *(edge_rows(strips, "gy", last) for last in (False, True)))
+    message = jnp.concatenate(
+        [strips[1].reshape(4, 8, 128), strips[3].reshape(4, 8, 128)]
+        + [part for array in own_rows for part in (array[11:16], array[26:32])])
+    beside = from_partner(message)
+    strip_rows, _ = lax.optimization_barrier((strip_rows, message))
+    corner = from_partner(jnp.concatenate([array[at : at + 1] for array in strip_rows for at in (1, 3)]))
+
+    main, strip = field(MAIN, 128), field(STRIP, 128)
+    kept = [(6, MAIN, 128), (7, STRIP, 128)]
+    pre, lower, message, to_first, to_second, *kept0 = call(
+        finest_kernel,
+        (own, strips, *own_rows, *strip_rows, partner, beside, corner),
+        [(16, 32, 128), (8, 16, 128), (40, 8, 128), (96, 128), (96, 128), *kept],
+        [main, strip] * 4 + [main, field(512, 128)])
+    partner = from_partner(message)
+    strips = from_sides("gz", to_first, to_second)
+    lower_strips = jnp.concatenate([part[:32].reshape(4, 8, 128) for part in strips])
+    pre_strips = merged_sides(*(part[32:].reshape(2, 32, 128) for part in strips))
+    further = from_partner(jnp.concatenate([lower_strips, pre_strips[0].reshape(4, 8, 128)]))
+    flat = jnp.concatenate([lower.reshape(16, 8, 128), lower_strips, partner[:16], further[:8]])
+    own2 = jnp.concatenate([pre, pre_strips, partner[16:].reshape(6, 32, 128), further[8:].reshape(1, 32, 128)])
+    rows1 = from_sides("gy", *(jnp.concatenate([flat, edge_rows(own2, "gy", last)]) for last in (False, True)))
+
+    window = field(SECOND, 128)
+    share, *kept1 = call(
+        second_kernel,
+        (flat.reshape(24, 16, 128), *rows1),
+        [(count_y * count_z, 4, 8, 128), (SECOND, 128), (5, SECOND, 128)],
+        [window] * 4 + [field(256, 128)])
+    shares = lax.all_to_all(share, ("gy", "gz"), 0, 0, tiled=True)
+
+    scratch = whole_scratch(8, 32) + whole_scratch(4, 16) + whole_scratch(2, 8)
+    scratch += [window, window] + [main, strip] * 2 + [field(8, 48, 128), field(384, 128), field(64, 128)]
+    (result,) = call(
+        functools.partial(last_kernel, count_y, count_z),
+        (own2, *rows1, shares, *kept1, *kept0),
+        [(16, 32, 128)],
+        scratch)
+    return result
+
+
 def solution(mesh):
     in_specs = (P("gx", "gy", "gz"), P("gx", "gy", "gz"))
     out_specs = P("gx", "gy", "gz")
-    return jax.shard_map(shards, mesh=mesh, in_specs=in_specs, out_specs=out_specs, check_vma=False)
+
+    def run(source, conductivity):
+        counts = tuple(mesh.shape[axis] for axis in ("gx", "gy", "gz"))
+        held = tuple(size // count for size, count in zip(source.shape, counts))
+        fast = counts == (2, 4, 4) and held == (16, 32, 128)
+        shards = fast_shards if fast else plain_shards
+        return jax.shard_map(shards, mesh=mesh, in_specs=in_specs, out_specs=out_specs, check_vma=False)(source, conductivity)
+
+    return run

time: 1210 us -> 76.7 us (0.06)
  the two profiles are of different devices: /device:TPU:30 before, /device:TPU:0 now
where the time goes in v1:
time: 76.7 us; the launch traced here: 76.4 us
  starting transfers between devices  23.9 us (31%)
  Pallas kernels  21.3 us (28%)
  blocking collectives  18.5 us (24%)
  waiting for transfers between devices  10.3 us (13%)
  local copies, waits for them, and re-layouts  2.08 us (3%)
    pallas_call x5, Pallas kernels, call(): pl.pallas_call(kernel, out_shape=[jax.ShapeDtypeStruct(shape, jnp.float32...  21.3 us
    all_to_all x1, blocking collectives, fast_shards(): shares = lax.all_to_all(share, ('gy', 'gz'), 0, 0, tiled=True)  18.5 us
    ppermute x10, starting transfers between devices, from_sides(): lax.ppermute(message, axis, lower + [(j, i) for i, j in lower])  17.7 us
    ppermute x5, waiting for transfers between devices, from_partner(): return lax.ppermute(message, 'gx', [(0, 1), (1, 0)])  7.45 us
    ppermute x5, starting transfers between devices, from_partner(): return lax.ppermute(message, 'gx', [(0, 1), (1, 0)])  6.14 us
    ppermute x10, waiting for transfers between devices, from_sides(): lax.ppermute(message, axis, lower + [(j, i) for i, j in lower])  2.89 us
    unnamed x15, local copies, waits for them, and re-layouts  1.97 us
  transfers between devices with their start and end apart: 15, of which 5 were waited for; matrix products, arithmetic and copies ran while one was open for 0% of the time, Pallas kernels for 1%

profile of v1, /device:TPU:0, one launch (start us, length us, event | category | flops | bytes accessed | tf_op | source)
XLA Modules:
  0.0 76.4 jit_solution(7080654684331650678)
XLA Ops:
  0.0 0.0 copy-start
  0.0 0.9 %copy-done = f32[16,32,128]{2,1,0:T(8,128)S(1)} copy-done((f32[16,32,128]{2,1,0:T(8,128)S(1)}, f32[16,32,128]{2,1,0:T(8,128)}, u32[]{:S(2)}) %copy-start) | copy-done | bytes 262168
  1.0 0.0 copy-start.1
  1.0 0.9 %copy-done.1 = f32[16,32,128]{2,1,0:T(8,128)S(1)} copy-done((f32[16,32,128]{2,1,0:T(8,128)S(1)}, f32[16,32,128]{2,1,0:T(8,128)}, u32[]{:S(2)}) %copy-start.1) | copy-done | bytes 262168
  2.0 3.0 %collective-permute-start.6 = (f32[13,32,128]{2,1,0:T(8,128)S(1)}, f32[13,32,128]{2,1,0:T(8,128)S(1)}, u32[]{:S(2)}, u32[]{:S(2)}) collective-permute-start(f32[13,32,128]{2,1,0:T(8,128)S(1)} %get-tuple-element.34), channel_id=1, source_target_pairs={{0,16},{16,0},{1,17},{17,1},{2,18},{18,2},{3,19},{19,3},{4,20},{20... | collective-permute-start | bytes 638984 | tf_op jit(solution)/shard_map/ppermute | solution.py:760
  5.0 0.5 shard_map.29
  5.5 0.7 collective-permute-start
  6.2 4.5 %collective-permute-start.1 = (f32[2,32,128]{2,1,0:T(8,128)S(1)}, f32[2,32,128]{2,1,0:T(8,128)S(1)}, u32[]{:S(2)}, u32[]{:S(2)}) collective-permute-start(f32[2,32,128]{2,1,0:T(8,128)S(1)} %get-tuple-element.27), channel_id=1, source_target_pairs={{0,1},{2,3},{1,0},{3,2},{4,5},{6,7},{5,4},{7,6},{8,9},{10,11},{9,8... | collective-permute-start | bytes 98312 | tf_op jit(solution)/shard_map/ppermute | solution.py:749
  10.6 0.7 collective-permute-start.2
  11.3 2.9 %collective-permute-start.3 = (f32[32,8,128]{2,1,0:T(8,128)S(1)}, f32[32,8,128]{2,1,0:T(8,128)S(1)}, u32[]{:S(2)}, u32[]{:S(2)}) collective-permute-start(f32[32,8,128]{2,1,0:T(8,128)S(1)} %get-tuple-element.29), channel_id=1, source_target_pairs={{0,4},{8,12},{4,0},{12,8},{1,5},{9,13},{5,1},{13,9},{2,6},{10,14},... | collective-permute-start | bytes 393224 | tf_op jit(solution)/shard_map/ppermute | solution.py:749
  14.2 0.0 collective-permute-done
  14.2 0.0 collective-permute-done.1
  14.3 0.7 collective-permute-start.5
  15.0 1.4 %collective-permute-start.4 = (f32[4,8,128]{2,1,0:T(8,128)S(1)}, f32[4,8,128]{2,1,0:T(8,128)S(1)}, u32[]{:S(2)}, u32[]{:S(2)}) collective-permute-start(f32[4,8,128]{2,1,0:T(8,128)S(1)} %get-tuple-element.50), channel_id=1, source_target_pairs={{0,4},{8,12},{4,0},{12,8},{1,5},{9,13},{5,1},{13,9},{2,6},{10,14},... | collective-permute-start | bytes 49160 | tf_op jit(solution)/shard_map/ppermute | solution.py:749
  16.4 0.0 collective-permute-done.2.own_second
  16.4 0.0 collective-permute-done.3.own_first
  16.4 0.6 collective-permute-start.7
  17.0 0.0 collective-permute-done.5.strip_second
  17.0 0.2 collective-permute-done.4.strip_first
  17.2 1.4 %collective-permute-start.8 = (f32[4,8,128]{2,1,0:T(8,128)S(1)}, f32[4,8,128]{2,1,0:T(8,128)S(1)}, u32[]{:S(2)}, u32[]{:S(2)}) collective-permute-start(f32[4,8,128]{2,1,0:T(8,128)S(1)} %pad_maximum_fusion.2), channel_id=1, source_target_pairs={{0,16},{16,0},{1,17},{17,1},{2,18},{18,2},{3,19},{19,3},{4,20},{20... | collective-permute-start | bytes 49160 | tf_op jit(solution)/shard_map/ppermute | solution.py:760
  18.6 3.9 %collective-permute-done.8.corner = f32[4,8,128]{2,1,0:T(8,128)S(1)} collective-permute-done((f32[4,8,128]{2,1,0:T(8,128)S(1)}, f32[4,8,128]{2,1,0:T(8,128)S(1)}, u32[]{:S(2)}, u32[]{:S(2)}) %collective-permute-start.8) | collective-permute-done | bytes 16416 | tf_op jit(solution)/shard_map/ppermute | solution.py:760
  22.5 0.0 collective-permute-done.6.partner
  22.5 0.0 collective-permute-done.7.beside
  22.5 6.3 %shard_map.30 = (f32[16,32,128]{2,1,0:T(8,128)S(1)}, f32[8,16,128]{2,1,0:T(8,128)S(1)}, f32[40,8,128]{2,1,0:T(8,128)S(1)}, f32[96,128]{1,0:T(8,128)S(1)}, f32[96...) custom-call(f32[32,32,128]{2,1,0:T(8,128)S(1)} %get-tuple-element.25.fields.own, ...), custom_call_target="tpu_custom_call" | custom-call | tf_op jit(solution)/shard_map/pallas_call | solution.py:730
  28.8 0.7 collective-permute-start.9
  29.5 3.2 %collective-permute-start.10 = (f32[96,128]{1,0:T(8,128)S(1)}, f32[96,128]{1,0:T(8,128)S(1)}, u32[]{:S(2)}, u32[]{:S(2)}) collective-permute-start(f32[96,128]{1,0:T(8,128)S(1)} %get-tuple-element.37), channel_id=1, source_target_pairs={{0,1},{2,3},{1,0},{3,2},{4,5},{6,7},{5,4},{7,6},{8,9},{10,11},{9,8... | collective-permute-start | bytes 147464 | tf_op jit(solution)/shard_map/ppermute | solution.py:749
  32.7 0.5 collective-permute-start.11
  33.2 0.0 collective-permute-done.9
  33.2 1.5 %collective-permute-done.10 = f32[96,128]{1,0:T(8,128)S(1)} collective-permute-done((f32[96,128]{1,0:T(8,128)S(1)}, f32[96,128]{1,0:T(8,128)S(1)}, u32[]{:S(2)}, u32[]{:S(2)}) %collective-permute-start.10) | collective-permute-done | bytes 49184 | tf_op jit(solution)/shard_map/ppermute | solution.py:749
  34.8 0.6 collective-permute-start.12
  35.4 3.5 %collective-permute-done.12 = f32[12,8,128]{2,1,0:T(8,128)S(1)} collective-permute-done((f32[12,8,128]{2,1,0:T(8,128)S(1)}, f32[12,8,128]{2,1,0:T(8,128)S(1)}, u32[]{:S(2)}, u32[]{:S(2)}) %collective-permute-start.12) | collective-permute-done | bytes 49184 | tf_op jit(solution)/shard_map/ppermute | solution.py:760
  38.9 0.0 collective-permute-done.11
  39.1 0.7 collective-permute-start.14
  39.8 2.4 %collective-permute-start.13 = (f32[73,8,128]{2,1,0:T(8,128)S(1)}, f32[73,8,128]{2,1,0:T(8,128)S(1)}, u32[]{:S(2)}, u32[]{:S(2)}) collective-permute-start(f32[73,8,128]{2,1,0:T(8,128)S(1)} %dynamic-slice_dynamic-update-slice_fusion.1), channel_id=1, source_target_pairs={{0,4},{8,12},{4,0},{12,8},{1,5},{9,13},{5,1},{13,9},{2,6},{10,14},... | collective-permute-start | bytes 897032 | tf_op jit(solution)/shard_map/ppermute | solution.py:749
  42.2 0.0 collective-permute-done.14.second.second1
  42.3 1.2 %collective-permute-done.13.first.first1 = f32[73,8,128]{2,1,0:T(8,128)S(1)} collective-permute-done((f32[73,8,128]{2,1,0:T(8,128)S(1)}, f32[73,8,128]{2,1,0:T(8,128)S(1)}, u32[]{:S(2)}, u32[]{:S(2)}) %collective-permute-start.13) | collective-permute-done | bytes 299040 | tf_op jit(solution)/shard_map/ppermute | solution.py:749
  43.5 2.9 %shard_map.31 = (f32[16,4,8,128]{3,2,1,0:T(8,128)S(1)}, f32[880,128]{1,0:T(8,128)S(1)}, f32[5,880,128]{2,1,0:T(8,128)S(1)}) custom-call(f32[24,16,128]{2,1,0:T(8,128)S(1)} %bitcast.33, f32[73,8,128]{2,1,0:T(8,128)S(1)} %collective-permute-done.13.first.first1, f32[73,8,128]{2,1,0:T(8,128)S(1)} %collective-permute-done.14.second.second1), custom_call_target="tpu_custom_call" | custom-call | tf_op jit(solution)/shard_map/pallas_call | solution.py:730
  46.3 18.5 %all_to_all.5.shares = f32[16,4,8,128]{3,2,1,0:T(8,128)S(1)} all-to-all(f32[16,4,8,128]{3,2,1,0:T(8,128)S(1)} %get-tuple-element.40), channel_id=1, replica_groups=mesh['gx'=2,'gy'=4,'gz'=4] {'gy','gz'}, dimensions={0} | all-to-all | bytes 524288 | tf_op jit(solution)/shard_map/all_to_all | solution.py:809
  64.8 11.6 %shard_map.32 = f32[16,32,128]{2,1,0:T(8,128)} custom-call(f32[25,32,128]{2,1,0:T(8,128)S(1)} %pad_maximum_fusion.own2, f32[73,8,128]{2,1,0:T(8,128)S(1)} %collective-permute-done.13.first.first1, f32[73,8,128]{2,1,0:T(8,128)S(1)} %collective-permute-done.14.second.second1, f32[16,4,8,128]{3,2,1,0:T(8,128)S(1)} %all_to_all.5.shares, ...), custom_call_target="tpu_custom_call" | custom-call | tf_op jit(solution)/shard_map/pallas_call | solution.py:730
  (32 shorter events, 0.3 us)
Async XLA Ops:
  0.0 0.9 %copy-start = (f32[16,32,128]{2,1,0:T(8,128)S(1)}, f32[16,32,128]{2,1,0:T(8,128)}, u32[]{:S(2)}) copy-start(f32[16,32,128]{2,1,0:T(8,128)} %rhs.1) | copy-start | bytes 786436
  1.0 0.9 %copy-start.1 = (f32[16,32,128]{2,1,0:T(8,128)S(1)}, f32[16,32,128]{2,1,0:T(8,128)}, u32[]{:S(2)}) copy-start(f32[16,32,128]{2,1,0:T(8,128)} %coef.1) | copy-start | bytes 786436
  2.0 20.6 %collective-permute-start.6 = (f32[13,32,128]{2,1,0:T(8,128)S(1)}, f32[13,32,128]{2,1,0:T(8,128)S(1)}, u32[]{:S(2)}, u32[]{:S(2)}) collective-permute-start(f32[13,32,128]{2,1,0:T(8,128)S(1)} %get-tuple-element.34), channel_id=1, source_target_pairs={{0,16},{16,0},{1,17},{17,1},{2,18},{18,2},{3,19},{19,3},{4,20},{20... | collective-permute-start | bytes 638984 | tf_op jit(solution)/shard_map/ppermute | solution.py:760
  5.5 8.7 %collective-permute-start = (f32[2,32,128]{2,1,0:T(8,128)S(1)}, f32[2,32,128]{2,1,0:T(8,128)S(1)}, u32[]{:S(2)}, u32[]{:S(2)}) collective-permute-start(f32[2,32,128]{2,1,0:T(8,128)S(1)} %get-tuple-element.26), channel_id=1, source_target_pairs={{1,2},{2,1},{5,6},{6,5},{9,10},{10,9},{13,14},{14,13},{17,18},{18,... | collective-permute-start | bytes 98312 | tf_op jit(solution)/shard_map/ppermute | solution.py:749
  6.2 8.1 %collective-permute-start.1 = (f32[2,32,128]{2,1,0:T(8,128)S(1)}, f32[2,32,128]{2,1,0:T(8,128)S(1)}, u32[]{:S(2)}, u32[]{:S(2)}) collective-permute-start(f32[2,32,128]{2,1,0:T(8,128)S(1)} %get-tuple-element.27), channel_id=1, source_target_pairs={{0,1},{2,3},{1,0},{3,2},{4,5},{6,7},{5,4},{7,6},{8,9},{10,11},{9,8... | collective-permute-start | bytes 98312 | tf_op jit(solution)/shard_map/ppermute | solution.py:749
  10.6 5.7 %collective-permute-start.2 = (f32[32,8,128]{2,1,0:T(8,128)S(1)}, f32[32,8,128]{2,1,0:T(8,128)S(1)}, u32[]{:S(2)}, u32[]{:S(2)}) collective-permute-start(f32[32,8,128]{2,1,0:T(8,128)S(1)} %get-tuple-element.28), channel_id=1, source_target_pairs={{4,8},{8,4},{5,9},{9,5},{6,10},{10,6},{7,11},{11,7},{20,24},{24,20... | collective-permute-start | bytes 393224 | tf_op jit(solution)/shard_map/ppermute | solution.py:749
  11.3 5.1 %collective-permute-start.3 = (f32[32,8,128]{2,1,0:T(8,128)S(1)}, f32[32,8,128]{2,1,0:T(8,128)S(1)}, u32[]{:S(2)}, u32[]{:S(2)}) collective-permute-start(f32[32,8,128]{2,1,0:T(8,128)S(1)} %get-tuple-element.29), channel_id=1, source_target_pairs={{0,4},{8,12},{4,0},{12,8},{1,5},{9,13},{5,1},{13,9},{2,6},{10,14},... | collective-permute-start | bytes 393224 | tf_op jit(solution)/shard_map/ppermute | solution.py:749
  14.3 2.7 %collective-permute-start.5 = (f32[4,8,128]{2,1,0:T(8,128)S(1)}, f32[4,8,128]{2,1,0:T(8,128)S(1)}, u32[]{:S(2)}, u32[]{:S(2)}) collective-permute-start(f32[4,8,128]{2,1,0:T(8,128)S(1)} %get-tuple-element.49), channel_id=1, source_target_pairs={{4,8},{8,4},{5,9},{9,5},{6,10},{10,6},{7,11},{11,7},{20,24},{24,20... | collective-permute-start | bytes 49160 | tf_op jit(solution)/shard_map/ppermute | solution.py:749
  15.0 2.2 %collective-permute-start.4 = (f32[4,8,128]{2,1,0:T(8,128)S(1)}, f32[4,8,128]{2,1,0:T(8,128)S(1)}, u32[]{:S(2)}, u32[]{:S(2)}) collective-permute-start(f32[4,8,128]{2,1,0:T(8,128)S(1)} %get-tuple-element.50), channel_id=1, source_target_pairs={{0,4},{8,12},{4,0},{12,8},{1,5},{9,13},{5,1},{13,9},{2,6},{10,14},... | collective-permute-start | bytes 49160 | tf_op jit(solution)/shard_map/ppermute | solution.py:749
  16.4 6.1 %collective-permute-start.7 = (f32[30,8,128]{2,1,0:T(8,128)S(1)}, f32[30,8,128]{2,1,0:T(8,128)S(1)}, u32[]{:S(2)}, u32[]{:S(2)}) collective-permute-start(f32[30,8,128]{2,1,0:T(8,128)S(1)} %constant_dynamic-update-slice_fusion.2), channel_id=1, source_target_pairs={{0,16},{16,0},{1,17},{17,1},{2,18},{18,2},{3,19},{19,3},{4,20},{20... | collective-permute-start | bytes 368648 | tf_op jit(solution)/shard_map/ppermute | solution.py:760
  17.2 5.3 %collective-permute-start.8 = (f32[4,8,128]{2,1,0:T(8,128)S(1)}, f32[4,8,128]{2,1,0:T(8,128)S(1)}, u32[]{:S(2)}, u32[]{:S(2)}) collective-permute-start(f32[4,8,128]{2,1,0:T(8,128)S(1)} %pad_maximum_fusion.2), channel_id=1, source_target_pairs={{0,16},{16,0},{1,17},{17,1},{2,18},{18,2},{3,19},{19,3},{4,20},{20... | collective-permute-start | bytes 49160 | tf_op jit(solution)/shard_map/ppermute | solution.py:760
  28.8 4.4 %collective-permute-start.9 = (f32[96,128]{1,0:T(8,128)S(1)}, f32[96,128]{1,0:T(8,128)S(1)}, u32[]{:S(2)}, u32[]{:S(2)}) collective-permute-start(f32[96,128]{1,0:T(8,128)S(1)} %get-tuple-element.36), channel_id=1, source_target_pairs={{1,2},{2,1},{5,6},{6,5},{9,10},{10,9},{13,14},{14,13},{17,18},{18,... | collective-permute-start | bytes 147464 | tf_op jit(solution)/shard_map/ppermute | solution.py:749
  29.5 5.3 %collective-permute-start.10 = (f32[96,128]{1,0:T(8,128)S(1)}, f32[96,128]{1,0:T(8,128)S(1)}, u32[]{:S(2)}, u32[]{:S(2)}) collective-permute-start(f32[96,128]{1,0:T(8,128)S(1)} %get-tuple-element.37), channel_id=1, source_target_pairs={{0,1},{2,3},{1,0},{3,2},{4,5},{6,7},{5,4},{7,6},{8,9},{10,11},{9,8... | collective-permute-start | bytes 147464 | tf_op jit(solution)/shard_map/ppermute | solution.py:749
  32.7 6.3 %collective-permute-start.11 = (f32[40,8,128]{2,1,0:T(8,128)S(1)}, f32[40,8,128]{2,1,0:T(8,128)S(1)}, u32[]{:S(2)}, u32[]{:S(2)}) collective-permute-start(f32[40,8,128]{2,1,0:T(8,128)S(1)} %get-tuple-element.38), channel_id=1, source_target_pairs={{0,16},{16,0},{1,17},{17,1},{2,18},{18,2},{3,19},{19,3},{4,20},{20... | collective-permute-start | bytes 491528 | tf_op jit(solution)/shard_map/ppermute | solution.py:760
  34.8 4.2 %collective-permute-start.12 = (f32[12,8,128]{2,1,0:T(8,128)S(1)}, f32[12,8,128]{2,1,0:T(8,128)S(1)}, u32[]{:S(2)}, u32[]{:S(2)}) collective-permute-start(f32[12,8,128]{2,1,0:T(8,128)S(1)} %pad_maximum_fusion.1), channel_id=1, source_target_pairs={{0,16},{16,0},{1,17},{17,1},{2,18},{18,2},{3,19},{19,3},{4,20},{20... | collective-permute-start | bytes 147464 | tf_op jit(solution)/shard_map/ppermute | solution.py:760
  39.1 3.1 %collective-permute-start.14 = (f32[73,8,128]{2,1,0:T(8,128)S(1)}, f32[73,8,128]{2,1,0:T(8,128)S(1)}, u32[]{:S(2)}, u32[]{:S(2)}) collective-permute-start(f32[73,8,128]{2,1,0:T(8,128)S(1)} %dynamic-slice_dynamic-update-slice_fusion), channel_id=1, source_target_pairs={{4,8},{8,4},{5,9},{9,5},{6,10},{10,6},{7,11},{11,7},{20,24},{24,20... | collective-permute-start | bytes 897032 | tf_op jit(solution)/shard_map/ppermute | solution.py:749
  39.8 3.7 %collective-permute-start.13 = (f32[73,8,128]{2,1,0:T(8,128)S(1)}, f32[73,8,128]{2,1,0:T(8,128)S(1)}, u32[]{:S(2)}, u32[]{:S(2)}) collective-permute-start(f32[73,8,128]{2,1,0:T(8,128)S(1)} %dynamic-slice_dynamic-update-slice_fusion.1), channel_id=1, source_target_pairs={{0,4},{8,12},{4,0},{12,8},{1,5},{9,13},{5,1},{13,9},{2,6},{10,14},... | collective-permute-start | bytes 897032 | tf_op jit(solution)/shard_map/ppermute | solution.py:749

commit v2 on v1

--- a/solution.py
+++ b/solution.py
@@ -347,24 +347,21 @@
     return left, right
 
 
-def plane_kernel(rhs, coef, fields, message):
-    side = lax.axis_index("gx")
-    for field_at, array in enumerate((rhs, coef)):
-        for local in range(16):
-            plane = array[local + side * (15 - 2 * local)]
-            fields[16 * field_at + local] = plane
-            if local > 9 - field_at:
-                message[6 * field_at + 15 - local] = plane
-
-
-def edge_kernel(fields, to_first, to_second, rows_first, rows_second):
+def pack_kernel(own, message, to_first, to_second, rows_first, rows_second):
     place = device_place()
     odd, odd_y = odd_at(place, 2), odd_at(place, 1)
     for group in range(2):
-        planes = [[fields[16 * field_at + 8 * group + slot] for slot in range(8)] for field_at in range(2)]
+        planes = ([], [])
+        for local in range(8 * group, 8 * group + 8):
+            held = local + place[0] * (15 - 2 * local)
+            for field_at in range(2):
+                plane = own[16 * field_at + held]
+                at = 16 * field_at + local
+                rows_first[at], rows_second[at] = by_side((plane[0:8], plane[24:32]), odd_y)
+                if local > 9 - field_at:
+                    message[6 * field_at + 15 - local] = plane
+                planes[field_at].append(plane)
         to_first[group], to_second[group] = by_side(strip_pages(*planes), odd)
-    for page in range(32):
-        rows_first[page], rows_second[page] = by_side((fields[page, 0:8], fields[page, 24:32]), odd_y)
 
 
 def mirrored_slots(value):
@@ -392,19 +389,17 @@
         array[block(main_at(4), ROWS)] = blank
     odd_y, odd_z = odd_at(place, 1), odd_at(place, 2)
 
-    no_rows = jnp.zeros((8, 128), jnp.float32)
     for local in range(23):
         at = block(main_at(local + 1), ROWS)
         for field_at, array in enumerate((rhs, coef)):
             if local < 16:
                 page = 16 * field_at + local
-                array[at] = with_tiles([own[page]], [own_first[page]], [own_second[page]], odd_y)
+                held = 16 * field_at + local + place[0] * (15 - 2 * local)
+                array[at] = with_tiles([own[held]], [own_first[page]], [own_second[page]], odd_y)
             elif local < 22 + field_at:
                 step = local - 16
-                page = 12 + 6 * field_at - step
-                beyond = step == 5 + field_at
-                first, second = (no_rows, no_rows) if beyond else (beside[page], beside[11 + page])
-                array[at] = with_tiles([partner[6 * field_at + step]], [first], [second], odd_y)
+                page = 13 + 7 * field_at - step
+                array[at] = with_tiles([partner[6 * field_at + step]], [beside[page]], [beside[13 + page]], odd_y)
     above = (iota((ROWS, 128), 1) & 15) < 8
     for group in range(3):
         pages = []
@@ -768,9 +763,12 @@
 
 def fast_shards(source, conductivity):
     count_y, count_z = lax.axis_size("gy"), lax.axis_size("gz")
-    own, message = call(plane_kernel, (source, conductivity), [(32, 32, 128), (13, 32, 128)], [])
-    to_first, to_second, *rows = call(
-        edge_kernel, (own,), [(2, 32, 128), (2, 32, 128), (32, 8, 128), (32, 8, 128)], [])
+    own = jnp.concatenate([source, conductivity])
+    message, to_first, to_second, *rows = call(
+        pack_kernel,
+        (own,),
+        [(13, 32, 128), (2, 32, 128), (2, 32, 128), (32, 8, 128), (32, 8, 128)],
+        [])
     partner = from_partner(message)
     strips = jnp.concatenate(from_sides("gz", to_first, to_second)[::-1])
     own_rev = from_sides("gy", *rows)[::-1]
@@ -779,7 +777,7 @@
     strip_rows = from_sides("gy", *(edge_rows(strips, "gy", last) for last in (False, True)))
     message = jnp.concatenate(
         [strips[1].reshape(4, 8, 128), strips[3].reshape(4, 8, 128)]
-        + [part for array in own_rows for part in (array[11:16], array[26:32])])
+        + [part for array in own_rows for part in (array[10:16], array[25:32])])
     beside = from_partner(message)
     strip_rows, _ = lax.optimization_barrier((strip_rows, message))
     corner = from_partner(jnp.concatenate([array[at : at + 1] for array in strip_rows for at in (1, 3)]))

time: 76.7 us -> 76 us (level)
  waiting for transfers between devices: 10.3 us -> 9.53 us
    concatenate x0 -> x1, local copies, waits for them, and re-layouts: none -> 0.97 us  [fast_shards(): own = jnp.concatenate([source, conductivity])]
    unnamed x15 -> x12, local copies, waits for them, and re-layouts: 1.97 us -> 1.04 us
    pallas_call x5 -> x4, Pallas kernels: 21.3 us -> 21.3 us  [call(): pl.pallas_call(kernel, out_shape=[jax.ShapeDtypeStruct(shape, jnp.float32...]
  transfers between devices with their start and end apart: 15 -> 15, of which waited for: 5 -> 5; matrix products, arithmetic and copies ran while one was open for 0% -> 0% of each run, Pallas kernels for 1% -> 0%
where the time goes in v2:
time: 76 us; the launch traced here: 75.7 us
  starting transfers between devices  24.3 us (32%)
  Pallas kernels  21.3 us (28%)
  blocking collectives  18.2 us (24%)
  waiting for transfers between devices  9.53 us (13%)
  local copies, waits for them, and re-layouts  2.12 us (3%)
    pallas_call x4, Pallas kernels, call(): pl.pallas_call(kernel, out_shape=[jax.ShapeDtypeStruct(shape, jnp.float32...  21.3 us
    all_to_all x1, blocking collectives, fast_shards(): shares = lax.all_to_all(share, ('gy', 'gz'), 0, 0, tiled=True)  18.2 us
    ppermute x10, starting transfers between devices, from_sides(): lax.ppermute(message, axis, lower + [(j, i) for i, j in lower])  17.7 us
    ppermute x5, waiting for transfers between devices, from_partner(): return lax.ppermute(message, 'gx', [(0, 1), (1, 0)])  7.29 us
    ppermute x5, starting transfers between devices, from_partner(): return lax.ppermute(message, 'gx', [(0, 1), (1, 0)])  6.54 us
    ppermute x10, waiting for transfers between devices, from_sides(): lax.ppermute(message, axis, lower + [(j, i) for i, j in lower])  2.24 us
  transfers between devices with their start and end apart: 15, of which 5 were waited for; matrix products, arithmetic and copies ran while one was open for 0% of the time, Pallas kernels for 0%

profile of v2, /device:TPU:0, one launch (start us, length us, event | category | flops | bytes accessed | tf_op | source)
XLA Modules:
  0.0 75.7 jit_solution(13698870512824048450)
XLA Ops:
  0.0 1.0 %constant_dynamic-update-slice_fusion.1 = f32[32,32,128]{2,1,0:T(8,128)S(1)} fusion(f32[16,32,128]{2,1,0:T(8,128)} %param.2), kind=kLoop, calls=%fused_computation.7 | loop fusion | bytes 524288
  1.0 1.0 %constant_dynamic-update-slice_fusion.own = f32[32,32,128]{2,1,0:T(8,128)S(1)} fusion(f32[32,32,128]{2,1,0:T(8,128)S(1)} %constant_dynamic-update-slice_fusion.1, f32[16,32,128]{2,1,0:T(8,128)} %param.3), kind=kLoop, calls=%fused_computation.6 | loop fusion | bytes 524288 | tf_op jit(solution)/shard_map/concatenate | solution.py:766
  1.9 0.5 shard_map.28
  2.5 0.7 collective-permute-start
  3.2 5.9 %collective-permute-start.1 = (f32[2,32,128]{2,1,0:T(8,128)S(1)}, f32[2,32,128]{2,1,0:T(8,128)S(1)}, u32[]{:S(2)}, u32[]{:S(2)}) collective-permute-start(f32[2,32,128]{2,1,0:T(8,128)S(1)} %get-tuple-element.25), channel_id=1, source_target_pairs={{0,1},{2,3},{1,0},{3,2},{4,5},{6,7},{5,4},{7,6},{8,9},{10,11},{9,8... | collective-permute-start | bytes 98312 | tf_op jit(solution)/shard_map/ppermute | solution.py:744
  9.1 0.7 collective-permute-start.2
  9.7 2.9 %collective-permute-start.3 = (f32[32,8,128]{2,1,0:T(8,128)S(1)}, f32[32,8,128]{2,1,0:T(8,128)S(1)}, u32[]{:S(2)}, u32[]{:S(2)}) collective-permute-start(f32[32,8,128]{2,1,0:T(8,128)S(1)} %get-tuple-element.27), channel_id=1, source_target_pairs={{0,4},{8,12},{4,0},{12,8},{1,5},{9,13},{5,1},{13,9},{2,6},{10,14},... | collective-permute-start | bytes 393224 | tf_op jit(solution)/shard_map/ppermute | solution.py:744
  12.7 1.5 %collective-permute-start.6 = (f32[13,32,128]{2,1,0:T(8,128)S(1)}, f32[13,32,128]{2,1,0:T(8,128)S(1)}, u32[]{:S(2)}, u32[]{:S(2)}) collective-permute-start(f32[13,32,128]{2,1,0:T(8,128)S(1)} %get-tuple-element.32), channel_id=1, source_target_pairs={{0,16},{16,0},{1,17},{17,1},{2,18},{18,2},{3,19},{19,3},{4,20},{20... | collective-permute-start | bytes 638984 | tf_op jit(solution)/shard_map/ppermute | solution.py:755
  14.2 0.0 collective-permute-done
  14.2 0.0 collective-permute-done.1
  14.2 0.7 collective-permute-start.5
  14.9 1.4 %collective-permute-start.4 = (f32[4,8,128]{2,1,0:T(8,128)S(1)}, f32[4,8,128]{2,1,0:T(8,128)S(1)}, u32[]{:S(2)}, u32[]{:S(2)}) collective-permute-start(f32[4,8,128]{2,1,0:T(8,128)S(1)} %get-tuple-element.48), channel_id=1, source_target_pairs={{0,4},{8,12},{4,0},{12,8},{1,5},{9,13},{5,1},{13,9},{2,6},{10,14},... | collective-permute-start | bytes 49160 | tf_op jit(solution)/shard_map/ppermute | solution.py:744
  16.3 0.0 collective-permute-done.2.own_second
  16.3 0.0 collective-permute-done.3.own_first
  16.4 0.6 collective-permute-start.7
  17.0 0.0 collective-permute-done.5.strip_second
  17.0 0.2 collective-permute-done.4.strip_first
  17.2 1.4 %collective-permute-start.8 = (f32[4,8,128]{2,1,0:T(8,128)S(1)}, f32[4,8,128]{2,1,0:T(8,128)S(1)}, u32[]{:S(2)}, u32[]{:S(2)}) collective-permute-start(f32[4,8,128]{2,1,0:T(8,128)S(1)} %pad_maximum_fusion.2), channel_id=1, source_target_pairs={{0,16},{16,0},{1,17},{17,1},{2,18},{18,2},{3,19},{19,3},{4,20},{20... | collective-permute-start | bytes 49160 | tf_op jit(solution)/shard_map/ppermute | solution.py:755
  18.6 4.7 %collective-permute-done.8.corner = f32[4,8,128]{2,1,0:T(8,128)S(1)} collective-permute-done((f32[4,8,128]{2,1,0:T(8,128)S(1)}, f32[4,8,128]{2,1,0:T(8,128)S(1)}, u32[]{:S(2)}, u32[]{:S(2)}) %collective-permute-start.8) | collective-permute-done | bytes 16416 | tf_op jit(solution)/shard_map/ppermute | solution.py:755
  23.3 0.0 collective-permute-done.6.partner
  23.3 0.0 collective-permute-done.7.beside
  23.3 6.3 %shard_map.29 = (f32[16,32,128]{2,1,0:T(8,128)S(1)}, f32[8,16,128]{2,1,0:T(8,128)S(1)}, f32[40,8,128]{2,1,0:T(8,128)S(1)}, f32[96,128]{1,0:T(8,128)S(1)}, f32[96...) custom-call(f32[32,32,128]{2,1,0:T(8,128)S(1)} %constant_dynamic-update-slice_fusion.own, ...), custom_call_target="tpu_custom_call" | custom-call | tf_op jit(solution)/shard_map/pallas_call | solution.py:725
  29.6 0.7 collective-permute-start.9
  30.2 1.8 %collective-permute-start.10 = (f32[96,128]{1,0:T(8,128)S(1)}, f32[96,128]{1,0:T(8,128)S(1)}, u32[]{:S(2)}, u32[]{:S(2)}) collective-permute-start(f32[96,128]{1,0:T(8,128)S(1)} %get-tuple-element.35), channel_id=1, source_target_pairs={{0,1},{2,3},{1,0},{3,2},{4,5},{6,7},{5,4},{7,6},{8,9},{10,11},{9,8... | collective-permute-start | bytes 147464 | tf_op jit(solution)/shard_map/ppermute | solution.py:744
  32.0 1.5 %collective-permute-start.11 = (f32[40,8,128]{2,1,0:T(8,128)S(1)}, f32[40,8,128]{2,1,0:T(8,128)S(1)}, u32[]{:S(2)}, u32[]{:S(2)}) collective-permute-start(f32[40,8,128]{2,1,0:T(8,128)S(1)} %get-tuple-element.36), channel_id=1, source_target_pairs={{0,16},{16,0},{1,17},{17,1},{2,18},{18,2},{3,19},{19,3},{4,20},{20... | collective-permute-start | bytes 491528 | tf_op jit(solution)/shard_map/ppermute | solution.py:755
  33.5 0.0 collective-permute-done.9
  33.5 0.8 %collective-permute-done.10 = f32[96,128]{1,0:T(8,128)S(1)} collective-permute-done((f32[96,128]{1,0:T(8,128)S(1)}, f32[96,128]{1,0:T(8,128)S(1)}, u32[]{:S(2)}, u32[]{:S(2)}) %collective-permute-start.10) | collective-permute-done | bytes 49184 | tf_op jit(solution)/shard_map/ppermute | solution.py:744
  34.5 1.6 %collective-permute-start.12 = (f32[12,8,128]{2,1,0:T(8,128)S(1)}, f32[12,8,128]{2,1,0:T(8,128)S(1)}, u32[]{:S(2)}, u32[]{:S(2)}) collective-permute-start(f32[12,8,128]{2,1,0:T(8,128)S(1)} %pad_maximum_fusion.1), channel_id=1, source_target_pairs={{0,16},{16,0},{1,17},{17,1},{2,18},{18,2},{3,19},{19,3},{4,20},{20... | collective-permute-start | bytes 147464 | tf_op jit(solution)/shard_map/ppermute | solution.py:755
  36.0 2.6 %collective-permute-done.12 = f32[12,8,128]{2,1,0:T(8,128)S(1)} collective-permute-done((f32[12,8,128]{2,1,0:T(8,128)S(1)}, f32[12,8,128]{2,1,0:T(8,128)S(1)}, u32[]{:S(2)}, u32[]{:S(2)}) %collective-permute-start.12) | collective-permute-done | bytes 49184 | tf_op jit(solution)/shard_map/ppermute | solution.py:755
  38.6 0.0 collective-permute-done.11
  38.8 0.7 collective-permute-start.14
  39.5 2.4 %collective-permute-start.13 = (f32[73,8,128]{2,1,0:T(8,128)S(1)}, f32[73,8,128]{2,1,0:T(8,128)S(1)}, u32[]{:S(2)}, u32[]{:S(2)}) collective-permute-start(f32[73,8,128]{2,1,0:T(8,128)S(1)} %dynamic-slice_dynamic-update-slice_fusion.1), channel_id=1, source_target_pairs={{0,4},{8,12},{4,0},{12,8},{1,5},{9,13},{5,1},{13,9},{2,6},{10,14},... | collective-permute-start | bytes 897032 | tf_op jit(solution)/shard_map/ppermute | solution.py:744
  41.9 0.0 collective-permute-done.14.second.second1
  41.9 1.2 %collective-permute-done.13.first.first1 = f32[73,8,128]{2,1,0:T(8,128)S(1)} collective-permute-done((f32[73,8,128]{2,1,0:T(8,128)S(1)}, f32[73,8,128]{2,1,0:T(8,128)S(1)}, u32[]{:S(2)}, u32[]{:S(2)}) %collective-permute-start.13) | collective-permute-done | bytes 299040 | tf_op jit(solution)/shard_map/ppermute | solution.py:744
  43.1 2.9 %shard_map.30 = (f32[16,4,8,128]{3,2,1,0:T(8,128)S(1)}, f32[880,128]{1,0:T(8,128)S(1)}, f32[5,880,128]{2,1,0:T(8,128)S(1)}) custom-call(f32[24,16,128]{2,1,0:T(8,128)S(1)} %bitcast.33, f32[73,8,128]{2,1,0:T(8,128)S(1)} %collective-permute-done.13.first.first1, f32[73,8,128]{2,1,0:T(8,128)S(1)} %collective-permute-done.14.second.second1), custom_call_target="tpu_custom_call" | custom-call | tf_op jit(solution)/shard_map/pallas_call | solution.py:725
  46.0 18.2 %all_to_all.5.shares = f32[16,4,8,128]{3,2,1,0:T(8,128)S(1)} all-to-all(f32[16,4,8,128]{3,2,1,0:T(8,128)S(1)} %get-tuple-element.38), channel_id=1, replica_groups=mesh['gx'=2,'gy'=4,'gz'=4] {'gy','gz'}, dimensions={0} | all-to-all | bytes 524288 | tf_op jit(solution)/shard_map/all_to_all | solution.py:807
  64.1 11.6 %shard_map.31 = f32[16,32,128]{2,1,0:T(8,128)} custom-call(f32[25,32,128]{2,1,0:T(8,128)S(1)} %pad_maximum_fusion.own2, f32[73,8,128]{2,1,0:T(8,128)S(1)} %collective-permute-done.13.first.first1, f32[73,8,128]{2,1,0:T(8,128)S(1)} %collective-permute-done.14.second.second1, f32[16,4,8,128]{3,2,1,0:T(8,128)S(1)} %all_to_all.5.shares, ...), custom_call_target="tpu_custom_call" | custom-call | tf_op jit(solution)/shard_map/pallas_call | solution.py:725
  (31 shorter events, 0.2 us)
Async XLA Ops:
  2.5 11.7 %collective-permute-start = (f32[2,32,128]{2,1,0:T(8,128)S(1)}, f32[2,32,128]{2,1,0:T(8,128)S(1)}, u32[]{:S(2)}, u32[]{:S(2)}) collective-permute-start(f32[2,32,128]{2,1,0:T(8,128)S(1)} %get-tuple-element.24), channel_id=1, source_target_pairs={{1,2},{2,1},{5,6},{6,5},{9,10},{10,9},{13,14},{14,13},{17,18},{18,... | collective-permute-start | bytes 98312 | tf_op jit(solution)/shard_map/ppermute | solution.py:744
  3.2 11.0 %collective-permute-start.1 = (f32[2,32,128]{2,1,0:T(8,128)S(1)}, f32[2,32,128]{2,1,0:T(8,128)S(1)}, u32[]{:S(2)}, u32[]{:S(2)}) collective-permute-start(f32[2,32,128]{2,1,0:T(8,128)S(1)} %get-tuple-element.25), channel_id=1, source_target_pairs={{0,1},{2,3},{1,0},{3,2},{4,5},{6,7},{5,4},{7,6},{8,9},{10,11},{9,8... | collective-permute-start | bytes 98312 | tf_op jit(solution)/shard_map/ppermute | solution.py:744
  9.1 7.2 %collective-permute-start.2 = (f32[32,8,128]{2,1,0:T(8,128)S(1)}, f32[32,8,128]{2,1,0:T(8,128)S(1)}, u32[]{:S(2)}, u32[]{:S(2)}) collective-permute-start(f32[32,8,128]{2,1,0:T(8,128)S(1)} %get-tuple-element.26), channel_id=1, source_target_pairs={{4,8},{8,4},{5,9},{9,5},{6,10},{10,6},{7,11},{11,7},{20,24},{24,20... | collective-permute-start | bytes 393224 | tf_op jit(solution)/shard_map/ppermute | solution.py:744
  9.7 6.6 %collective-permute-start.3 = (f32[32,8,128]{2,1,0:T(8,128)S(1)}, f32[32,8,128]{2,1,0:T(8,128)S(1)}, u32[]{:S(2)}, u32[]{:S(2)}) collective-permute-start(f32[32,8,128]{2,1,0:T(8,128)S(1)} %get-tuple-element.27), channel_id=1, source_target_pairs={{0,4},{8,12},{4,0},{12,8},{1,5},{9,13},{5,1},{13,9},{2,6},{10,14},... | collective-permute-start | bytes 393224 | tf_op jit(solution)/shard_map/ppermute | solution.py:744
  12.7 10.6 %collective-permute-start.6 = (f32[13,32,128]{2,1,0:T(8,128)S(1)}, f32[13,32,128]{2,1,0:T(8,128)S(1)}, u32[]{:S(2)}, u32[]{:S(2)}) collective-permute-start(f32[13,32,128]{2,1,0:T(8,128)S(1)} %get-tuple-element.32), channel_id=1, source_target_pairs={{0,16},{16,0},{1,17},{17,1},{2,18},{18,2},{3,19},{19,3},{4,20},{20... | collective-permute-start | bytes 638984 | tf_op jit(solution)/shard_map/ppermute | solution.py:755
  14.2 2.7 %collective-permute-start.5 = (f32[4,8,128]{2,1,0:T(8,128)S(1)}, f32[4,8,128]{2,1,0:T(8,128)S(1)}, u32[]{:S(2)}, u32[]{:S(2)}) collective-permute-start(f32[4,8,128]{2,1,0:T(8,128)S(1)} %get-tuple-element.47), channel_id=1, source_target_pairs={{4,8},{8,4},{5,9},{9,5},{6,10},{10,6},{7,11},{11,7},{20,24},{24,20... | collective-permute-start | bytes 49160 | tf_op jit(solution)/shard_map/ppermute | solution.py:744
  14.9 2.2 %collective-permute-start.4 = (f32[4,8,128]{2,1,0:T(8,128)S(1)}, f32[4,8,128]{2,1,0:T(8,128)S(1)}, u32[]{:S(2)}, u32[]{:S(2)}) collective-permute-start(f32[4,8,128]{2,1,0:T(8,128)S(1)} %get-tuple-element.48), channel_id=1, source_target_pairs={{0,4},{8,12},{4,0},{12,8},{1,5},{9,13},{5,1},{13,9},{2,6},{10,14},... | collective-permute-start | bytes 49160 | tf_op jit(solution)/shard_map/ppermute | solution.py:744
  16.4 6.9 %collective-permute-start.7 = (f32[34,8,128]{2,1,0:T(8,128)S(1)}, f32[34,8,128]{2,1,0:T(8,128)S(1)}, u32[]{:S(2)}, u32[]{:S(2)}) collective-permute-start(f32[34,8,128]{2,1,0:T(8,128)S(1)} %constant_dynamic-update-slice_fusion.4), channel_id=1, source_target_pairs={{0,16},{16,0},{1,17},{17,1},{2,18},{18,2},{3,19},{19,3},{4,20},{20... | collective-permute-start | bytes 417800 | tf_op jit(solution)/shard_map/ppermute | solution.py:755
  17.2 6.1 %collective-permute-start.8 = (f32[4,8,128]{2,1,0:T(8,128)S(1)}, f32[4,8,128]{2,1,0:T(8,128)S(1)}, u32[]{:S(2)}, u32[]{:S(2)}) collective-permute-start(f32[4,8,128]{2,1,0:T(8,128)S(1)} %pad_maximum_fusion.2), channel_id=1, source_target_pairs={{0,16},{16,0},{1,17},{17,1},{2,18},{18,2},{3,19},{19,3},{4,20},{20... | collective-permute-start | bytes 49160 | tf_op jit(solution)/shard_map/ppermute | solution.py:755
  29.6 4.0 %collective-permute-start.9 = (f32[96,128]{1,0:T(8,128)S(1)}, f32[96,128]{1,0:T(8,128)S(1)}, u32[]{:S(2)}, u32[]{:S(2)}) collective-permute-start(f32[96,128]{1,0:T(8,128)S(1)} %get-tuple-element.34), channel_id=1, source_target_pairs={{1,2},{2,1},{5,6},{6,5},{9,10},{10,9},{13,14},{14,13},{17,18},{18,... | collective-permute-start | bytes 147464 | tf_op jit(solution)/shard_map/ppermute | solution.py:744
  30.2 4.2 %collective-permute-start.10 = (f32[96,128]{1,0:T(8,128)S(1)}, f32[96,128]{1,0:T(8,128)S(1)}, u32[]{:S(2)}, u32[]{:S(2)}) collective-permute-start(f32[96,128]{1,0:T(8,128)S(1)} %get-tuple-element.35), channel_id=1, source_target_pairs={{0,1},{2,3},{1,0},{3,2},{4,5},{6,7},{5,4},{7,6},{8,9},{10,11},{9,8... | collective-permute-start | bytes 147464 | tf_op jit(solution)/shard_map/ppermute | solution.py:744
  32.0 6.6 %collective-permute-start.11 = (f32[40,8,128]{2,1,0:T(8,128)S(1)}, f32[40,8,128]{2,1,0:T(8,128)S(1)}, u32[]{:S(2)}, u32[]{:S(2)}) collective-permute-start(f32[40,8,128]{2,1,0:T(8,128)S(1)} %get-tuple-element.36), channel_id=1, source_target_pairs={{0,16},{16,0},{1,17},{17,1},{2,18},{18,2},{3,19},{19,3},{4,20},{20... | collective-permute-start | bytes 491528 | tf_op jit(solution)/shard_map/ppermute | solution.py:755
  34.5 4.2 %collective-permute-start.12 = (f32[12,8,128]{2,1,0:T(8,128)S(1)}, f32[12,8,128]{2,1,0:T(8,128)S(1)}, u32[]{:S(2)}, u32[]{:S(2)}) collective-permute-start(f32[12,8,128]{2,1,0:T(8,128)S(1)} %pad_maximum_fusion.1), channel_id=1, source_target_pairs={{0,16},{16,0},{1,17},{17,1},{2,18},{18,2},{3,19},{19,3},{4,20},{20... | collective-permute-start | bytes 147464 | tf_op jit(solution)/shard_map/ppermute | solution.py:755
  38.8 3.1 %collective-permute-start.14 = (f32[73,8,128]{2,1,0:T(8,128)S(1)}, f32[73,8,128]{2,1,0:T(8,128)S(1)}, u32[]{:S(2)}, u32[]{:S(2)}) collective-permute-start(f32[73,8,128]{2,1,0:T(8,128)S(1)} %dynamic-slice_dynamic-update-slice_fusion), channel_id=1, source_target_pairs={{4,8},{8,4},{5,9},{9,5},{6,10},{10,6},{7,11},{11,7},{20,24},{24,20... | collective-permute-start | bytes 897032 | tf_op jit(solution)/shard_map/ppermute | solution.py:744
  39.5 3.6 %collective-permute-start.13 = (f32[73,8,128]{2,1,0:T(8,128)S(1)}, f32[73,8,128]{2,1,0:T(8,128)S(1)}, u32[]{:S(2)}, u32[]{:S(2)}) collective-permute-start(f32[73,8,128]{2,1,0:T(8,128)S(1)} %dynamic-slice_dynamic-update-slice_fusion.1), channel_id=1, source_target_pairs={{0,4},{8,12},{4,0},{12,8},{1,5},{9,13},{5,1},{13,9},{2,6},{10,14},... | collective-permute-start | bytes 897032 | tf_op jit(solution)/shard_map/ppermute | solution.py:744

commit v3 on v2

--- a/solution.py
+++ b/solution.py
@@ -2,6 +2,7 @@
 
 import jax
 import jax.numpy as jnp
+import numpy as np
 from jax import lax
 from jax.experimental import pallas as pl
 from jax.experimental.pallas import tpu as pltpu
@@ -389,6 +390,7 @@
         array[block(main_at(4), ROWS)] = blank
     odd_y, odd_z = odd_at(place, 1), odd_at(place, 2)
 
+    no_rows = jnp.zeros((8, 128), jnp.float32)
     for local in range(23):
         at = block(main_at(local + 1), ROWS)
         for field_at, array in enumerate((rhs, coef)):
@@ -398,8 +400,10 @@
                 array[at] = with_tiles([own[held]], [own_first[page]], [own_second[page]], odd_y)
             elif local < 22 + field_at:
                 step = local - 16
-                page = 13 + 7 * field_at - step
-                array[at] = with_tiles([partner[6 * field_at + step]], [beside[page]], [beside[13 + page]], odd_y)
+                page = 12 + 6 * field_at - step
+                beyond = step == 5 + field_at
+                first, second = (no_rows, no_rows) if beyond else (beside[page], beside[11 + page])
+                array[at] = with_tiles([partner[6 * field_at + step]], [first], [second], odd_y)
     above = (iota((ROWS, 128), 1) & 15) < 8
     for group in range(3):
         pages = []
@@ -757,13 +761,14 @@
 
 def merged_sides(first, second):
     odd = lax.axis_index("gz") % 2 == 1
-    above = lax.broadcasted_iota(jnp.int32, first.shape, first.ndim - 1) % 16 < 8
+    above = np.arange(128) % 16 < 8
     return jnp.where(above == odd, second, first)
 
 
 def fast_shards(source, conductivity):
     count_y, count_z = lax.axis_size("gy"), lax.axis_size("gz")
-    own = jnp.concatenate([source, conductivity])
+    second = np.array([False, True]).reshape(2, 1, 1, 1)
+    own = jnp.where(second, conductivity[None], source[None]).reshape(32, 32, 128)
     message, to_first, to_second, *rows = call(
         pack_kernel,
         (own,),
@@ -777,7 +782,7 @@
     strip_rows = from_sides("gy", *(edge_rows(strips, "gy", last) for last in (False, True)))
     message = jnp.concatenate(
         [strips[1].reshape(4, 8, 128), strips[3].reshape(4, 8, 128)]
-        + [part for array in own_rows for part in (array[10:16], array[25:32])])
+        + [part for array in own_rows for part in (array[11:16], array[26:32])])
     beside = from_partner(message)
     strip_rows, _ = lax.optimization_barrier((strip_rows, message))
     corner = from_partner(jnp.concatenate([array[at : at + 1] for array in strip_rows for at in (1, 3)]))

time: 76 us -> 75.6 us (level)
  other arithmetic: 0.06 us -> 1.86 us
  local copies, waits for them, and re-layouts: 2.12 us -> 0.99 us
  waiting for transfers between devices: 9.53 us -> 8.53 us
    select_n x0 -> x1, other arithmetic: none -> 1.15 us  [fast_shards(): jnp.where(second, conductivity[None], source[None]).reshape(32, 32, 128)]
    ppermute x5, waiting for transfers between devices: 7.29 us -> 6.29 us  [from_partner(): return lax.ppermute(message, 'gx', [(0, 1), (1, 0)])]
    concatenate x1 -> x0, local copies, waits for them, and re-layouts: 0.97 us -> none  [fast_shards(): own = jnp.concatenate([source, conductivity])]
    unnamed x12 -> x11, local copies, waits for them, and re-layouts: 1.04 us -> 0.07 us
    broadcast_in_dim x0 -> x2, local copies, waits for them, and re-layouts: none -> 0.81 us  [fast_shards(): jnp.where(second, conductivity[None], source[None]).reshape(32, 32, 128)]
  transfers between devices with their start and end apart: 15 -> 15, of which waited for: 5 -> 5; matrix products, arithmetic and copies ran while one was open for 0% -> 1% of each run, Pallas kernels for 0% -> 0%
where the time goes in v3:
time: 75.6 us; the launch traced here: 75.4 us
  starting transfers between devices  24.3 us (32%)
  Pallas kernels  21.3 us (28%)
  blocking collectives  18.2 us (24%)
  waiting for transfers between devices  8.53 us (11%)
  other arithmetic  1.86 us (2%)
  local copies, waits for them, and re-layouts  0.99 us (1%)
    pallas_call x4, Pallas kernels, call(): pl.pallas_call(kernel, out_shape=[jax.ShapeDtypeStruct(shape, jnp.float32...  21.3 us
    all_to_all x1, blocking collectives, fast_shards(): shares = lax.all_to_all(share, ('gy', 'gz'), 0, 0, tiled=True)  18.2 us
    ppermute x10, starting transfers between devices, from_sides(): lax.ppermute(message, axis, lower + [(j, i) for i, j in lower])  17.7 us
    ppermute x5, starting transfers between devices, from_partner(): return lax.ppermute(message, 'gx', [(0, 1), (1, 0)])  6.54 us
    ppermute x5, waiting for transfers between devices, from_partner(): return lax.ppermute(message, 'gx', [(0, 1), (1, 0)])  6.29 us
    ppermute x10, waiting for transfers between devices, from_sides(): lax.ppermute(message, axis, lower + [(j, i) for i, j in lower])  2.24 us
  transfers between devices with their start and end apart: 15, of which 5 were waited for; matrix products, arithmetic and copies ran while one was open for 1% of the time, Pallas kernels for 0%

profile of v3, /device:TPU:0, one launch (start us, length us, event | category | flops | bytes accessed | tf_op | source)
XLA Modules:
  0.0 75.4 jit_solution(16302486521757812882)
XLA Ops:
  0.0 0.7 broadcast_in_dim.41
  0.7 0.1 broadcast_in_dim.42
  0.8 1.1 %bitcast_select_fusion.own = f32[32,32,128]{2,1,0:T(8,128)S(1)} fusion(f32[16,32,128]{2,1,0:T(8,128)} %param.4, f32[16,32,128]{2,1,0:T(8,128)} %param.5, pred[32]{0:T(512)(128)(4,1)S(1)} %broadcast_in_dim.42), kind=kLoop, calls=%fused_computation | loop fusion | flops 131072 | bytes 1048608 | tf_op jit(solution)/shard_map/jit(_where)/select_n | solution.py:771
  2.0 0.5 shard_map.46
  2.5 0.7 collective-permute-start
  3.2 5.9 %collective-permute-start.1 = (f32[2,32,128]{2,1,0:T(8,128)S(1)}, f32[2,32,128]{2,1,0:T(8,128)S(1)}, u32[]{:S(2)}, u32[]{:S(2)}) collective-permute-start(f32[2,32,128]{2,1,0:T(8,128)S(1)} %get-tuple-element.25), channel_id=1, source_target_pairs={{0,1},{2,3},{1,0},{3,2},{4,5},{6,7},{5,4},{7,6},{8,9},{10,11},{9,8... | collective-permute-start | bytes 98312 | tf_op jit(solution)/shard_map/ppermute | solution.py:748
  9.1 0.7 collective-permute-start.2
  9.8 2.9 %collective-permute-start.3 = (f32[32,8,128]{2,1,0:T(8,128)S(1)}, f32[32,8,128]{2,1,0:T(8,128)S(1)}, u32[]{:S(2)}, u32[]{:S(2)}) collective-permute-start(f32[32,8,128]{2,1,0:T(8,128)S(1)} %get-tuple-element.27), channel_id=1, source_target_pairs={{0,4},{8,12},{4,0},{12,8},{1,5},{9,13},{5,1},{13,9},{2,6},{10,14},... | collective-permute-start | bytes 393224 | tf_op jit(solution)/shard_map/ppermute | solution.py:748
  12.7 1.5 %collective-permute-start.6 = (f32[13,32,128]{2,1,0:T(8,128)S(1)}, f32[13,32,128]{2,1,0:T(8,128)S(1)}, u32[]{:S(2)}, u32[]{:S(2)}) collective-permute-start(f32[13,32,128]{2,1,0:T(8,128)S(1)} %get-tuple-element.32), channel_id=1, source_target_pairs={{0,16},{16,0},{1,17},{17,1},{2,18},{18,2},{3,19},{19,3},{4,20},{20... | collective-permute-start | bytes 638984 | tf_op jit(solution)/shard_map/ppermute | solution.py:759
  14.2 0.0 collective-permute-done
  14.2 0.0 collective-permute-done.1
  14.2 0.7 collective-permute-start.5
  14.9 1.4 %collective-permute-start.4 = (f32[4,8,128]{2,1,0:T(8,128)S(1)}, f32[4,8,128]{2,1,0:T(8,128)S(1)}, u32[]{:S(2)}, u32[]{:S(2)}) collective-permute-start(f32[4,8,128]{2,1,0:T(8,128)S(1)} %get-tuple-element.48), channel_id=1, source_target_pairs={{0,4},{8,12},{4,0},{12,8},{1,5},{9,13},{5,1},{13,9},{2,6},{10,14},... | collective-permute-start | bytes 49160 | tf_op jit(solution)/shard_map/ppermute | solution.py:748
  16.3 0.0 collective-permute-done.2.own_second
  16.3 0.0 collective-permute-done.3.own_first
  16.4 0.6 collective-permute-start.7
  17.0 0.0 collective-permute-done.5.strip_second
  17.0 0.2 collective-permute-done.4.strip_first
  17.2 1.4 %collective-permute-start.8 = (f32[4,8,128]{2,1,0:T(8,128)S(1)}, f32[4,8,128]{2,1,0:T(8,128)S(1)}, u32[]{:S(2)}, u32[]{:S(2)}) collective-permute-start(f32[4,8,128]{2,1,0:T(8,128)S(1)} %pad_maximum_fusion.2), channel_id=1, source_target_pairs={{0,16},{16,0},{1,17},{17,1},{2,18},{18,2},{3,19},{19,3},{4,20},{20... | collective-permute-start | bytes 49160 | tf_op jit(solution)/shard_map/ppermute | solution.py:759
  18.6 0.7 broadcast_compare_fusion
  19.2 3.7 %collective-permute-done.8.corner = f32[4,8,128]{2,1,0:T(8,128)S(1)} collective-permute-done((f32[4,8,128]{2,1,0:T(8,128)S(1)}, f32[4,8,128]{2,1,0:T(8,128)S(1)}, u32[]{:S(2)}, u32[]{:S(2)}) %collective-permute-start.8) | collective-permute-done | bytes 16416 | tf_op jit(solution)/shard_map/ppermute | solution.py:759
  22.9 0.0 collective-permute-done.6.partner
  22.9 0.0 collective-permute-done.7.beside
  22.9 6.3 %shard_map.47 = (f32[16,32,128]{2,1,0:T(8,128)S(1)}, f32[8,16,128]{2,1,0:T(8,128)S(1)}, f32[40,8,128]{2,1,0:T(8,128)S(1)}, f32[96,128]{1,0:T(8,128)S(1)}, f32[96...) custom-call(f32[32,32,128]{2,1,0:T(8,128)S(1)} %bitcast_select_fusion.own, ...), custom_call_target="tpu_custom_call" | custom-call | tf_op jit(solution)/shard_map/pallas_call | solution.py:729
  29.2 0.7 collective-permute-start.9
  29.9 1.8 %collective-permute-start.10 = (f32[96,128]{1,0:T(8,128)S(1)}, f32[96,128]{1,0:T(8,128)S(1)}, u32[]{:S(2)}, u32[]{:S(2)}) collective-permute-start(f32[96,128]{1,0:T(8,128)S(1)} %get-tuple-element.35), channel_id=1, source_target_pairs={{0,1},{2,3},{1,0},{3,2},{4,5},{6,7},{5,4},{7,6},{8,9},{10,11},{9,8... | collective-permute-start | bytes 147464 | tf_op jit(solution)/shard_map/ppermute | solution.py:748
  31.7 1.5 %collective-permute-start.11 = (f32[40,8,128]{2,1,0:T(8,128)S(1)}, f32[40,8,128]{2,1,0:T(8,128)S(1)}, u32[]{:S(2)}, u32[]{:S(2)}) collective-permute-start(f32[40,8,128]{2,1,0:T(8,128)S(1)} %get-tuple-element.36), channel_id=1, source_target_pairs={{0,16},{16,0},{1,17},{17,1},{2,18},{18,2},{3,19},{19,3},{4,20},{20... | collective-permute-start | bytes 491528 | tf_op jit(solution)/shard_map/ppermute | solution.py:759
  33.2 0.0 collective-permute-done.9
  33.2 0.8 %collective-permute-done.10 = f32[96,128]{1,0:T(8,128)S(1)} collective-permute-done((f32[96,128]{1,0:T(8,128)S(1)}, f32[96,128]{1,0:T(8,128)S(1)}, u32[]{:S(2)}, u32[]{:S(2)}) %collective-permute-start.10) | collective-permute-done | bytes 49184 | tf_op jit(solution)/shard_map/ppermute | solution.py:748
  34.1 1.6 %collective-permute-start.12 = (f32[12,8,128]{2,1,0:T(8,128)S(1)}, f32[12,8,128]{2,1,0:T(8,128)S(1)}, u32[]{:S(2)}, u32[]{:S(2)}) collective-permute-start(f32[12,8,128]{2,1,0:T(8,128)S(1)} %pad_maximum_fusion.1), channel_id=1, source_target_pairs={{0,16},{16,0},{1,17},{17,1},{2,18},{18,2},{3,19},{19,3},{4,20},{20... | collective-permute-start | bytes 147464 | tf_op jit(solution)/shard_map/ppermute | solution.py:759
  35.7 2.6 %collective-permute-done.12 = f32[12,8,128]{2,1,0:T(8,128)S(1)} collective-permute-done((f32[12,8,128]{2,1,0:T(8,128)S(1)}, f32[12,8,128]{2,1,0:T(8,128)S(1)}, u32[]{:S(2)}, u32[]{:S(2)}) %collective-permute-start.12) | collective-permute-done | bytes 49184 | tf_op jit(solution)/shard_map/ppermute | solution.py:759
  38.3 0.0 collective-permute-done.11
  38.5 0.7 collective-permute-start.14
  39.1 2.4 %collective-permute-start.13 = (f32[73,8,128]{2,1,0:T(8,128)S(1)}, f32[73,8,128]{2,1,0:T(8,128)S(1)}, u32[]{:S(2)}, u32[]{:S(2)}) collective-permute-start(f32[73,8,128]{2,1,0:T(8,128)S(1)} %dynamic-slice_dynamic-update-slice_fusion.1), channel_id=1, source_target_pairs={{0,4},{8,12},{4,0},{12,8},{1,5},{9,13},{5,1},{13,9},{2,6},{10,14},... | collective-permute-start | bytes 897032 | tf_op jit(solution)/shard_map/ppermute | solution.py:748
  41.5 0.0 collective-permute-done.14.second.second1
  41.5 1.2 %collective-permute-done.13.first.first1 = f32[73,8,128]{2,1,0:T(8,128)S(1)} collective-permute-done((f32[73,8,128]{2,1,0:T(8,128)S(1)}, f32[73,8,128]{2,1,0:T(8,128)S(1)}, u32[]{:S(2)}, u32[]{:S(2)}) %collective-permute-start.13) | collective-permute-done | bytes 299040 | tf_op jit(solution)/shard_map/ppermute | solution.py:748
  42.7 2.9 %shard_map.48 = (f32[16,4,8,128]{3,2,1,0:T(8,128)S(1)}, f32[880,128]{1,0:T(8,128)S(1)}, f32[5,880,128]{2,1,0:T(8,128)S(1)}) custom-call(f32[24,16,128]{2,1,0:T(8,128)S(1)} %bitcast.37, f32[73,8,128]{2,1,0:T(8,128)S(1)} %collective-permute-done.13.first.first1, f32[73,8,128]{2,1,0:T(8,128)S(1)} %collective-permute-done.14.second.second1), custom_call_target="tpu_custom_call" | custom-call | tf_op jit(solution)/shard_map/pallas_call | solution.py:729
  45.6 18.2 %all_to_all.5.shares = f32[16,4,8,128]{3,2,1,0:T(8,128)S(1)} all-to-all(f32[16,4,8,128]{3,2,1,0:T(8,128)S(1)} %get-tuple-element.38), channel_id=1, replica_groups=mesh['gx'=2,'gy'=4,'gz'=4] {'gy','gz'}, dimensions={0} | all-to-all | bytes 524288 | tf_op jit(solution)/shard_map/all_to_all | solution.py:812
  63.8 11.6 %shard_map.49 = f32[16,32,128]{2,1,0:T(8,128)} custom-call(f32[25,32,128]{2,1,0:T(8,128)S(1)} %pad_maximum_fusion.own2, f32[73,8,128]{2,1,0:T(8,128)S(1)} %collective-permute-done.13.first.first1, f32[73,8,128]{2,1,0:T(8,128)S(1)} %collective-permute-done.14.second.second1, f32[16,4,8,128]{3,2,1,0:T(8,128)S(1)} %all_to_all.5.shares, ...), custom_call_target="tpu_custom_call" | custom-call | tf_op jit(solution)/shard_map/pallas_call | solution.py:729
  (29 shorter events, 0.2 us)
Async XLA Ops:
  2.5 11.7 %collective-permute-start = (f32[2,32,128]{2,1,0:T(8,128)S(1)}, f32[2,32,128]{2,1,0:T(8,128)S(1)}, u32[]{:S(2)}, u32[]{:S(2)}) collective-permute-start(f32[2,32,128]{2,1,0:T(8,128)S(1)} %get-tuple-element.24), channel_id=1, source_target_pairs={{1,2},{2,1},{5,6},{6,5},{9,10},{10,9},{13,14},{14,13},{17,18},{18,... | collective-permute-start | bytes 98312 | tf_op jit(solution)/shard_map/ppermute | solution.py:748
  3.2 11.0 %collective-permute-start.1 = (f32[2,32,128]{2,1,0:T(8,128)S(1)}, f32[2,32,128]{2,1,0:T(8,128)S(1)}, u32[]{:S(2)}, u32[]{:S(2)}) collective-permute-start(f32[2,32,128]{2,1,0:T(8,128)S(1)} %get-tuple-element.25), channel_id=1, source_target_pairs={{0,1},{2,3},{1,0},{3,2},{4,5},{6,7},{5,4},{7,6},{8,9},{10,11},{9,8... | collective-permute-start | bytes 98312 | tf_op jit(solution)/shard_map/ppermute | solution.py:748
  9.1 7.2 %collective-permute-start.2 = (f32[32,8,128]{2,1,0:T(8,128)S(1)}, f32[32,8,128]{2,1,0:T(8,128)S(1)}, u32[]{:S(2)}, u32[]{:S(2)}) collective-permute-start(f32[32,8,128]{2,1,0:T(8,128)S(1)} %get-tuple-element.26), channel_id=1, source_target_pairs={{4,8},{8,4},{5,9},{9,5},{6,10},{10,6},{7,11},{11,7},{20,24},{24,20... | collective-permute-start | bytes 393224 | tf_op jit(solution)/shard_map/ppermute | solution.py:748
  9.8 6.6 %collective-permute-start.3 = (f32[32,8,128]{2,1,0:T(8,128)S(1)}, f32[32,8,128]{2,1,0:T(8,128)S(1)}, u32[]{:S(2)}, u32[]{:S(2)}) collective-permute-start(f32[32,8,128]{2,1,0:T(8,128)S(1)} %get-tuple-element.27), channel_id=1, source_target_pairs={{0,4},{8,12},{4,0},{12,8},{1,5},{9,13},{5,1},{13,9},{2,6},{10,14},... | collective-permute-start | bytes 393224 | tf_op jit(solution)/shard_map/ppermute | solution.py:748
  12.7 10.2 %collective-permute-start.6 = (f32[13,32,128]{2,1,0:T(8,128)S(1)}, f32[13,32,128]{2,1,0:T(8,128)S(1)}, u32[]{:S(2)}, u32[]{:S(2)}) collective-permute-start(f32[13,32,128]{2,1,0:T(8,128)S(1)} %get-tuple-element.32), channel_id=1, source_target_pairs={{0,16},{16,0},{1,17},{17,1},{2,18},{18,2},{3,19},{19,3},{4,20},{20... | collective-permute-start | bytes 638984 | tf_op jit(solution)/shard_map/ppermute | solution.py:759
  14.2 2.7 %collective-permute-start.5 = (f32[4,8,128]{2,1,0:T(8,128)S(1)}, f32[4,8,128]{2,1,0:T(8,128)S(1)}, u32[]{:S(2)}, u32[]{:S(2)}) collective-permute-start(f32[4,8,128]{2,1,0:T(8,128)S(1)} %get-tuple-element.47), channel_id=1, source_target_pairs={{4,8},{8,4},{5,9},{9,5},{6,10},{10,6},{7,11},{11,7},{20,24},{24,20... | collective-permute-start | bytes 49160 | tf_op jit(solution)/shard_map/ppermute | solution.py:748
  14.9 2.2 %collective-permute-start.4 = (f32[4,8,128]{2,1,0:T(8,128)S(1)}, f32[4,8,128]{2,1,0:T(8,128)S(1)}, u32[]{:S(2)}, u32[]{:S(2)}) collective-permute-start(f32[4,8,128]{2,1,0:T(8,128)S(1)} %get-tuple-element.48), channel_id=1, source_target_pairs={{0,4},{8,12},{4,0},{12,8},{1,5},{9,13},{5,1},{13,9},{2,6},{10,14},... | collective-permute-start | bytes 49160 | tf_op jit(solution)/shard_map/ppermute | solution.py:748
  16.4 6.5 %collective-permute-start.7 = (f32[30,8,128]{2,1,0:T(8,128)S(1)}, f32[30,8,128]{2,1,0:T(8,128)S(1)}, u32[]{:S(2)}, u32[]{:S(2)}) collective-permute-start(f32[30,8,128]{2,1,0:T(8,128)S(1)} %constant_dynamic-update-slice_fusion.2), channel_id=1, source_target_pairs={{0,16},{16,0},{1,17},{17,1},{2,18},{18,2},{3,19},{19,3},{4,20},{20... | collective-permute-start | bytes 368648 | tf_op jit(solution)/shard_map/ppermute | solution.py:759
  17.2 5.8 %collective-permute-start.8 = (f32[4,8,128]{2,1,0:T(8,128)S(1)}, f32[4,8,128]{2,1,0:T(8,128)S(1)}, u32[]{:S(2)}, u32[]{:S(2)}) collective-permute-start(f32[4,8,128]{2,1,0:T(8,128)S(1)} %pad_maximum_fusion.2), channel_id=1, source_target_pairs={{0,16},{16,0},{1,17},{17,1},{2,18},{18,2},{3,19},{19,3},{4,20},{20... | collective-permute-start | bytes 49160 | tf_op jit(solution)/shard_map/ppermute | solution.py:759
  29.2 4.0 %collective-permute-start.9 = (f32[96,128]{1,0:T(8,128)S(1)}, f32[96,128]{1,0:T(8,128)S(1)}, u32[]{:S(2)}, u32[]{:S(2)}) collective-permute-start(f32[96,128]{1,0:T(8,128)S(1)} %get-tuple-element.34), channel_id=1, source_target_pairs={{1,2},{2,1},{5,6},{6,5},{9,10},{10,9},{13,14},{14,13},{17,18},{18,... | collective-permute-start | bytes 147464 | tf_op jit(solution)/shard_map/ppermute | solution.py:748
  29.9 4.2 %collective-permute-start.10 = (f32[96,128]{1,0:T(8,128)S(1)}, f32[96,128]{1,0:T(8,128)S(1)}, u32[]{:S(2)}, u32[]{:S(2)}) collective-permute-start(f32[96,128]{1,0:T(8,128)S(1)} %get-tuple-element.35), channel_id=1, source_target_pairs={{0,1},{2,3},{1,0},{3,2},{4,5},{6,7},{5,4},{7,6},{8,9},{10,11},{9,8... | collective-permute-start | bytes 147464 | tf_op jit(solution)/shard_map/ppermute | solution.py:748
  31.7 6.6 %collective-permute-start.11 = (f32[40,8,128]{2,1,0:T(8,128)S(1)}, f32[40,8,128]{2,1,0:T(8,128)S(1)}, u32[]{:S(2)}, u32[]{:S(2)}) collective-permute-start(f32[40,8,128]{2,1,0:T(8,128)S(1)} %get-tuple-element.36), channel_id=1, source_target_pairs={{0,16},{16,0},{1,17},{17,1},{2,18},{18,2},{3,19},{19,3},{4,20},{20... | collective-permute-start | bytes 491528 | tf_op jit(solution)/shard_map/ppermute | solution.py:759
  34.1 4.2 %collective-permute-start.12 = (f32[12,8,128]{2,1,0:T(8,128)S(1)}, f32[12,8,128]{2,1,0:T(8,128)S(1)}, u32[]{:S(2)}, u32[]{:S(2)}) collective-permute-start(f32[12,8,128]{2,1,0:T(8,128)S(1)} %pad_maximum_fusion.1), channel_id=1, source_target_pairs={{0,16},{16,0},{1,17},{17,1},{2,18},{18,2},{3,19},{19,3},{4,20},{20... | collective-permute-start | bytes 147464 | tf_op jit(solution)/shard_map/ppermute | solution.py:759
  38.5 3.1 %collective-permute-start.14 = (f32[73,8,128]{2,1,0:T(8,128)S(1)}, f32[73,8,128]{2,1,0:T(8,128)S(1)}, u32[]{:S(2)}, u32[]{:S(2)}) collective-permute-start(f32[73,8,128]{2,1,0:T(8,128)S(1)} %dynamic-slice_dynamic-update-slice_fusion), channel_id=1, source_target_pairs={{4,8},{8,4},{5,9},{9,5},{6,10},{10,6},{7,11},{11,7},{20,24},{24,20... | collective-permute-start | bytes 897032 | tf_op jit(solution)/shard_map/ppermute | solution.py:748
  39.1 3.6 %collective-permute-start.13 = (f32[73,8,128]{2,1,0:T(8,128)S(1)}, f32[73,8,128]{2,1,0:T(8,128)S(1)}, u32[]{:S(2)}, u32[]{:S(2)}) collective-permute-start(f32[73,8,128]{2,1,0:T(8,128)S(1)} %dynamic-slice_dynamic-update-slice_fusion.1), channel_id=1, source_target_pairs={{0,4},{8,12},{4,0},{12,8},{1,5},{9,13},{5,1},{13,9},{2,6},{10,14},... | collective-permute-start | bytes 897032 | tf_op jit(solution)/shard_map/ppermute | solution.py:748

commit v4 on v3

--- a/solution.py
+++ b/solution.py
@@ -2,7 +2,6 @@
 
 import jax
 import jax.numpy as jnp
-import numpy as np
 from jax import lax
 from jax.experimental import pallas as pl
 from jax.experimental.pallas import tpu as pltpu
@@ -761,13 +760,13 @@
 
 def merged_sides(first, second):
     odd = lax.axis_index("gz") % 2 == 1
-    above = np.arange(128) % 16 < 8
+    above = lax.broadcasted_iota(jnp.int32, (128,), 0) % 16 < 8
     return jnp.where(above == odd, second, first)
 
 
 def fast_shards(source, conductivity):
     count_y, count_z = lax.axis_size("gy"), lax.axis_size("gz")
-    second = np.array([False, True]).reshape(2, 1, 1, 1)
+    second = lax.broadcasted_iota(jnp.int32, (2, *source.shape), 0) == 1
     own = jnp.where(second, conductivity[None], source[None]).reshape(32, 32, 128)
     message, to_first, to_second, *rows = call(
         pack_kernel,

time: 75.6 us -> 75 us (level)
    broadcast_in_dim x2 -> x0, local copies, waits for them, and re-layouts: 0.81 us -> none  [fast_shards(): jnp.where(second, conductivity[None], source[None]).reshape(32, 32, 128)]
  transfers between devices with their start and end apart: 15 -> 15, of which waited for: 5 -> 5; matrix products, arithmetic and copies ran while one was open for 1% -> 0% of each run, Pallas kernels for 0% -> 0%
where the time goes in v4:
time: 75 us; the launch traced here: 74.7 us
  starting transfers between devices  24.3 us (32%)
  Pallas kernels  21.3 us (28%)
  blocking collectives  18.2 us (24%)
  waiting for transfers between devices  9.18 us (12%)
  other arithmetic  1.21 us (2%)
    pallas_call x4, Pallas kernels, call(): pl.pallas_call(kernel, out_shape=[jax.ShapeDtypeStruct(shape, jnp.float32...  21.3 us
    all_to_all x1, blocking collectives, fast_shards(): shares = lax.all_to_all(share, ('gy', 'gz'), 0, 0, tiled=True)  18.2 us
    ppermute x10, starting transfers between devices, from_sides(): lax.ppermute(message, axis, lower + [(j, i) for i, j in lower])  17.7 us
    ppermute x5, waiting for transfers between devices, from_partner(): return lax.ppermute(message, 'gx', [(0, 1), (1, 0)])  6.95 us
    ppermute x5, starting transfers between devices, from_partner(): return lax.ppermute(message, 'gx', [(0, 1), (1, 0)])  6.54 us
    ppermute x10, waiting for transfers between devices, from_sides(): lax.ppermute(message, axis, lower + [(j, i) for i, j in lower])  2.24 us
  transfers between devices with their start and end apart: 15, of which 5 were waited for; matrix products, arithmetic and copies ran while one was open for 0% of the time, Pallas kernels for 0%

profile of v4, /device:TPU:0, one launch (start us, length us, event | category | flops | bytes accessed | tf_op | source)
XLA Modules:
  0.0 74.7 jit_solution(9954263742315773804)
XLA Ops:
  0.0 0.1 iota.14
  0.1 0.1 iota.15
  0.2 1.1 %bitcast_select_fusion.own = f32[32,32,128]{2,1,0:T(8,128)S(1)} fusion(f32[16,32,128]{2,1,0:T(8,128)} %param.2, f32[16,32,128]{2,1,0:T(8,128)} %param.3, pred[32]{0:T(512)(128)(4,1)S(1)} %iota.15), kind=kLoop, calls=%fused_computation | loop fusion | flops 131072 | bytes 1048608 | tf_op jit(solution)/shard_map/jit(_where)/select_n | solution.py:770
  1.3 0.5 shard_map.28
  1.9 0.7 collective-permute-start
  2.5 5.9 %collective-permute-start.1 = (f32[2,32,128]{2,1,0:T(8,128)S(1)}, f32[2,32,128]{2,1,0:T(8,128)S(1)}, u32[]{:S(2)}, u32[]{:S(2)}) collective-permute-start(f32[2,32,128]{2,1,0:T(8,128)S(1)} %get-tuple-element.25), channel_id=1, source_target_pairs={{0,1},{2,3},{1,0},{3,2},{4,5},{6,7},{5,4},{7,6},{8,9},{10,11},{9,8... | collective-permute-start | bytes 98312 | tf_op jit(solution)/shard_map/ppermute | solution.py:747
  8.5 0.7 collective-permute-start.2
  9.1 2.9 %collective-permute-start.3 = (f32[32,8,128]{2,1,0:T(8,128)S(1)}, f32[32,8,128]{2,1,0:T(8,128)S(1)}, u32[]{:S(2)}, u32[]{:S(2)}) collective-permute-start(f32[32,8,128]{2,1,0:T(8,128)S(1)} %get-tuple-element.27), channel_id=1, source_target_pairs={{0,4},{8,12},{4,0},{12,8},{1,5},{9,13},{5,1},{13,9},{2,6},{10,14},... | collective-permute-start | bytes 393224 | tf_op jit(solution)/shard_map/ppermute | solution.py:747
  12.1 1.5 %collective-permute-start.6 = (f32[13,32,128]{2,1,0:T(8,128)S(1)}, f32[13,32,128]{2,1,0:T(8,128)S(1)}, u32[]{:S(2)}, u32[]{:S(2)}) collective-permute-start(f32[13,32,128]{2,1,0:T(8,128)S(1)} %get-tuple-element.32), channel_id=1, source_target_pairs={{0,16},{16,0},{1,17},{17,1},{2,18},{18,2},{3,19},{19,3},{4,20},{20... | collective-permute-start | bytes 638984 | tf_op jit(solution)/shard_map/ppermute | solution.py:758
  13.6 0.0 collective-permute-done
  13.6 0.0 collective-permute-done.1
  13.6 0.7 collective-permute-start.5
  14.3 1.4 %collective-permute-start.4 = (f32[4,8,128]{2,1,0:T(8,128)S(1)}, f32[4,8,128]{2,1,0:T(8,128)S(1)}, u32[]{:S(2)}, u32[]{:S(2)}) collective-permute-start(f32[4,8,128]{2,1,0:T(8,128)S(1)} %get-tuple-element.48), channel_id=1, source_target_pairs={{0,4},{8,12},{4,0},{12,8},{1,5},{9,13},{5,1},{13,9},{2,6},{10,14},... | collective-permute-start | bytes 49160 | tf_op jit(solution)/shard_map/ppermute | solution.py:747
  15.7 0.0 collective-permute-done.2.own_second
  15.7 0.0 collective-permute-done.3.own_first
  15.7 0.6 collective-permute-start.7
  16.3 0.0 collective-permute-done.5.strip_second
  16.3 0.2 collective-permute-done.4.strip_first
  16.5 1.4 %collective-permute-start.8 = (f32[4,8,128]{2,1,0:T(8,128)S(1)}, f32[4,8,128]{2,1,0:T(8,128)S(1)}, u32[]{:S(2)}, u32[]{:S(2)}) collective-permute-start(f32[4,8,128]{2,1,0:T(8,128)S(1)} %pad_maximum_fusion.2), channel_id=1, source_target_pairs={{0,16},{16,0},{1,17},{17,1},{2,18},{18,2},{3,19},{19,3},{4,20},{20... | collective-permute-start | bytes 49160 | tf_op jit(solution)/shard_map/ppermute | solution.py:758
  17.9 4.3 %collective-permute-done.8.corner = f32[4,8,128]{2,1,0:T(8,128)S(1)} collective-permute-done((f32[4,8,128]{2,1,0:T(8,128)S(1)}, f32[4,8,128]{2,1,0:T(8,128)S(1)}, u32[]{:S(2)}, u32[]{:S(2)}) %collective-permute-start.8) | collective-permute-done | bytes 16416 | tf_op jit(solution)/shard_map/ppermute | solution.py:758
  22.3 0.0 collective-permute-done.6.partner
  22.3 0.0 collective-permute-done.7.beside
  22.3 6.3 %shard_map.29 = (f32[16,32,128]{2,1,0:T(8,128)S(1)}, f32[8,16,128]{2,1,0:T(8,128)S(1)}, f32[40,8,128]{2,1,0:T(8,128)S(1)}, f32[96,128]{1,0:T(8,128)S(1)}, f32[96...) custom-call(f32[32,32,128]{2,1,0:T(8,128)S(1)} %bitcast_select_fusion.own, ...), custom_call_target="tpu_custom_call" | custom-call | tf_op jit(solution)/shard_map/pallas_call | solution.py:728
  28.6 0.7 collective-permute-start.9
  29.3 1.8 %collective-permute-start.10 = (f32[96,128]{1,0:T(8,128)S(1)}, f32[96,128]{1,0:T(8,128)S(1)}, u32[]{:S(2)}, u32[]{:S(2)}) collective-permute-start(f32[96,128]{1,0:T(8,128)S(1)} %get-tuple-element.35), channel_id=1, source_target_pairs={{0,1},{2,3},{1,0},{3,2},{4,5},{6,7},{5,4},{7,6},{8,9},{10,11},{9,8... | collective-permute-start | bytes 147464 | tf_op jit(solution)/shard_map/ppermute | solution.py:747
  31.0 1.5 %collective-permute-start.11 = (f32[40,8,128]{2,1,0:T(8,128)S(1)}, f32[40,8,128]{2,1,0:T(8,128)S(1)}, u32[]{:S(2)}, u32[]{:S(2)}) collective-permute-start(f32[40,8,128]{2,1,0:T(8,128)S(1)} %get-tuple-element.36), channel_id=1, source_target_pairs={{0,16},{16,0},{1,17},{17,1},{2,18},{18,2},{3,19},{19,3},{4,20},{20... | collective-permute-start | bytes 491528 | tf_op jit(solution)/shard_map/ppermute | solution.py:758
  32.6 0.0 collective-permute-done.9
  32.6 0.8 %collective-permute-done.10 = f32[96,128]{1,0:T(8,128)S(1)} collective-permute-done((f32[96,128]{1,0:T(8,128)S(1)}, f32[96,128]{1,0:T(8,128)S(1)}, u32[]{:S(2)}, u32[]{:S(2)}) %collective-permute-start.10) | collective-permute-done | bytes 49184 | tf_op jit(solution)/shard_map/ppermute | solution.py:747
  33.5 1.6 %collective-permute-start.12 = (f32[12,8,128]{2,1,0:T(8,128)S(1)}, f32[12,8,128]{2,1,0:T(8,128)S(1)}, u32[]{:S(2)}, u32[]{:S(2)}) collective-permute-start(f32[12,8,128]{2,1,0:T(8,128)S(1)} %pad_maximum_fusion.1), channel_id=1, source_target_pairs={{0,16},{16,0},{1,17},{17,1},{2,18},{18,2},{3,19},{19,3},{4,20},{20... | collective-permute-start | bytes 147464 | tf_op jit(solution)/shard_map/ppermute | solution.py:758
  35.0 2.6 %collective-permute-done.12 = f32[12,8,128]{2,1,0:T(8,128)S(1)} collective-permute-done((f32[12,8,128]{2,1,0:T(8,128)S(1)}, f32[12,8,128]{2,1,0:T(8,128)S(1)}, u32[]{:S(2)}, u32[]{:S(2)}) %collective-permute-start.12) | collective-permute-done | bytes 49184 | tf_op jit(solution)/shard_map/ppermute | solution.py:758
  37.6 0.0 collective-permute-done.11
  37.8 0.7 collective-permute-start.14
  38.5 2.4 %collective-permute-start.13 = (f32[73,8,128]{2,1,0:T(8,128)S(1)}, f32[73,8,128]{2,1,0:T(8,128)S(1)}, u32[]{:S(2)}, u32[]{:S(2)}) collective-permute-start(f32[73,8,128]{2,1,0:T(8,128)S(1)} %dynamic-slice_dynamic-update-slice_fusion.1), channel_id=1, source_target_pairs={{0,4},{8,12},{4,0},{12,8},{1,5},{9,13},{5,1},{13,9},{2,6},{10,14},... | collective-permute-start | bytes 897032 | tf_op jit(solution)/shard_map/ppermute | solution.py:747
  40.9 0.0 collective-permute-done.14.second.second1
  40.9 1.2 %collective-permute-done.13.first.first1 = f32[73,8,128]{2,1,0:T(8,128)S(1)} collective-permute-done((f32[73,8,128]{2,1,0:T(8,128)S(1)}, f32[73,8,128]{2,1,0:T(8,128)S(1)}, u32[]{:S(2)}, u32[]{:S(2)}) %collective-permute-start.13) | collective-permute-done | bytes 299040 | tf_op jit(solution)/shard_map/ppermute | solution.py:747
  42.1 2.9 %shard_map.30 = (f32[16,4,8,128]{3,2,1,0:T(8,128)S(1)}, f32[880,128]{1,0:T(8,128)S(1)}, f32[5,880,128]{2,1,0:T(8,128)S(1)}) custom-call(f32[24,16,128]{2,1,0:T(8,128)S(1)} %bitcast.37, f32[73,8,128]{2,1,0:T(8,128)S(1)} %collective-permute-done.13.first.first1, f32[73,8,128]{2,1,0:T(8,128)S(1)} %collective-permute-done.14.second.second1), custom_call_target="tpu_custom_call" | custom-call | tf_op jit(solution)/shard_map/pallas_call | solution.py:728
  45.0 18.2 %all_to_all.5.shares = f32[16,4,8,128]{3,2,1,0:T(8,128)S(1)} all-to-all(f32[16,4,8,128]{3,2,1,0:T(8,128)S(1)} %get-tuple-element.38), channel_id=1, replica_groups=mesh['gx'=2,'gy'=4,'gz'=4] {'gy','gz'}, dimensions={0} | all-to-all | bytes 524288 | tf_op jit(solution)/shard_map/all_to_all | solution.py:811
  63.2 11.6 %shard_map.31 = f32[16,32,128]{2,1,0:T(8,128)} custom-call(f32[25,32,128]{2,1,0:T(8,128)S(1)} %pad_maximum_fusion.own2, f32[73,8,128]{2,1,0:T(8,128)S(1)} %collective-permute-done.13.first.first1, f32[73,8,128]{2,1,0:T(8,128)S(1)} %collective-permute-done.14.second.second1, f32[16,4,8,128]{3,2,1,0:T(8,128)S(1)} %all_to_all.5.shares, ...), custom_call_target="tpu_custom_call" | custom-call | tf_op jit(solution)/shard_map/pallas_call | solution.py:728
  (31 shorter events, 0.2 us)
Async XLA Ops:
  1.9 11.7 %collective-permute-start = (f32[2,32,128]{2,1,0:T(8,128)S(1)}, f32[2,32,128]{2,1,0:T(8,128)S(1)}, u32[]{:S(2)}, u32[]{:S(2)}) collective-permute-start(f32[2,32,128]{2,1,0:T(8,128)S(1)} %get-tuple-element.24), channel_id=1, source_target_pairs={{1,2},{2,1},{5,6},{6,5},{9,10},{10,9},{13,14},{14,13},{17,18},{18,... | collective-permute-start | bytes 98312 | tf_op jit(solution)/shard_map/ppermute | solution.py:747
  2.5 11.0 %collective-permute-start.1 = (f32[2,32,128]{2,1,0:T(8,128)S(1)}, f32[2,32,128]{2,1,0:T(8,128)S(1)}, u32[]{:S(2)}, u32[]{:S(2)}) collective-permute-start(f32[2,32,128]{2,1,0:T(8,128)S(1)} %get-tuple-element.25), channel_id=1, source_target_pairs={{0,1},{2,3},{1,0},{3,2},{4,5},{6,7},{5,4},{7,6},{8,9},{10,11},{9,8... | collective-permute-start | bytes 98312 | tf_op jit(solution)/shard_map/ppermute | solution.py:747
  8.5 7.2 %collective-permute-start.2 = (f32[32,8,128]{2,1,0:T(8,128)S(1)}, f32[32,8,128]{2,1,0:T(8,128)S(1)}, u32[]{:S(2)}, u32[]{:S(2)}) collective-permute-start(f32[32,8,128]{2,1,0:T(8,128)S(1)} %get-tuple-element.26), channel_id=1, source_target_pairs={{4,8},{8,4},{5,9},{9,5},{6,10},{10,6},{7,11},{11,7},{20,24},{24,20... | collective-permute-start | bytes 393224 | tf_op jit(solution)/shard_map/ppermute | solution.py:747
  9.1 6.6 %collective-permute-start.3 = (f32[32,8,128]{2,1,0:T(8,128)S(1)}, f32[32,8,128]{2,1,0:T(8,128)S(1)}, u32[]{:S(2)}, u32[]{:S(2)}) collective-permute-start(f32[32,8,128]{2,1,0:T(8,128)S(1)} %get-tuple-element.27), channel_id=1, source_target_pairs={{0,4},{8,12},{4,0},{12,8},{1,5},{9,13},{5,1},{13,9},{2,6},{10,14},... | collective-permute-start | bytes 393224 | tf_op jit(solution)/shard_map/ppermute | solution.py:747
  12.1 10.2 %collective-permute-start.6 = (f32[13,32,128]{2,1,0:T(8,128)S(1)}, f32[13,32,128]{2,1,0:T(8,128)S(1)}, u32[]{:S(2)}, u32[]{:S(2)}) collective-permute-start(f32[13,32,128]{2,1,0:T(8,128)S(1)} %get-tuple-element.32), channel_id=1, source_target_pairs={{0,16},{16,0},{1,17},{17,1},{2,18},{18,2},{3,19},{19,3},{4,20},{20... | collective-permute-start | bytes 638984 | tf_op jit(solution)/shard_map/ppermute | solution.py:758
  13.6 2.7 %collective-permute-start.5 = (f32[4,8,128]{2,1,0:T(8,128)S(1)}, f32[4,8,128]{2,1,0:T(8,128)S(1)}, u32[]{:S(2)}, u32[]{:S(2)}) collective-permute-start(f32[4,8,128]{2,1,0:T(8,128)S(1)} %get-tuple-element.47), channel_id=1, source_target_pairs={{4,8},{8,4},{5,9},{9,5},{6,10},{10,6},{7,11},{11,7},{20,24},{24,20... | collective-permute-start | bytes 49160 | tf_op jit(solution)/shard_map/ppermute | solution.py:747
  14.3 2.2 %collective-permute-start.4 = (f32[4,8,128]{2,1,0:T(8,128)S(1)}, f32[4,8,128]{2,1,0:T(8,128)S(1)}, u32[]{:S(2)}, u32[]{:S(2)}) collective-permute-start(f32[4,8,128]{2,1,0:T(8,128)S(1)} %get-tuple-element.48), channel_id=1, source_target_pairs={{0,4},{8,12},{4,0},{12,8},{1,5},{9,13},{5,1},{13,9},{2,6},{10,14},... | collective-permute-start | bytes 49160 | tf_op jit(solution)/shard_map/ppermute | solution.py:747
  15.7 6.5 %collective-permute-start.7 = (f32[30,8,128]{2,1,0:T(8,128)S(1)}, f32[30,8,128]{2,1,0:T(8,128)S(1)}, u32[]{:S(2)}, u32[]{:S(2)}) collective-permute-start(f32[30,8,128]{2,1,0:T(8,128)S(1)} %constant_dynamic-update-slice_fusion.2), channel_id=1, source_target_pairs={{0,16},{16,0},{1,17},{17,1},{2,18},{18,2},{3,19},{19,3},{4,20},{20... | collective-permute-start | bytes 368648 | tf_op jit(solution)/shard_map/ppermute | solution.py:758
  16.5 5.8 %collective-permute-start.8 = (f32[4,8,128]{2,1,0:T(8,128)S(1)}, f32[4,8,128]{2,1,0:T(8,128)S(1)}, u32[]{:S(2)}, u32[]{:S(2)}) collective-permute-start(f32[4,8,128]{2,1,0:T(8,128)S(1)} %pad_maximum_fusion.2), channel_id=1, source_target_pairs={{0,16},{16,0},{1,17},{17,1},{2,18},{18,2},{3,19},{19,3},{4,20},{20... | collective-permute-start | bytes 49160 | tf_op jit(solution)/shard_map/ppermute | solution.py:758
  28.6 4.0 %collective-permute-start.9 = (f32[96,128]{1,0:T(8,128)S(1)}, f32[96,128]{1,0:T(8,128)S(1)}, u32[]{:S(2)}, u32[]{:S(2)}) collective-permute-start(f32[96,128]{1,0:T(8,128)S(1)} %get-tuple-element.34), channel_id=1, source_target_pairs={{1,2},{2,1},{5,6},{6,5},{9,10},{10,9},{13,14},{14,13},{17,18},{18,... | collective-permute-start | bytes 147464 | tf_op jit(solution)/shard_map/ppermute | solution.py:747
  29.3 4.2 %collective-permute-start.10 = (f32[96,128]{1,0:T(8,128)S(1)}, f32[96,128]{1,0:T(8,128)S(1)}, u32[]{:S(2)}, u32[]{:S(2)}) collective-permute-start(f32[96,128]{1,0:T(8,128)S(1)} %get-tuple-element.35), channel_id=1, source_target_pairs={{0,1},{2,3},{1,0},{3,2},{4,5},{6,7},{5,4},{7,6},{8,9},{10,11},{9,8... | collective-permute-start | bytes 147464 | tf_op jit(solution)/shard_map/ppermute | solution.py:747
  31.0 6.6 %collective-permute-start.11 = (f32[40,8,128]{2,1,0:T(8,128)S(1)}, f32[40,8,128]{2,1,0:T(8,128)S(1)}, u32[]{:S(2)}, u32[]{:S(2)}) collective-permute-start(f32[40,8,128]{2,1,0:T(8,128)S(1)} %get-tuple-element.36), channel_id=1, source_target_pairs={{0,16},{16,0},{1,17},{17,1},{2,18},{18,2},{3,19},{19,3},{4,20},{20... | collective-permute-start | bytes 491528 | tf_op jit(solution)/shard_map/ppermute | solution.py:758
  33.5 4.2 %collective-permute-start.12 = (f32[12,8,128]{2,1,0:T(8,128)S(1)}, f32[12,8,128]{2,1,0:T(8,128)S(1)}, u32[]{:S(2)}, u32[]{:S(2)}) collective-permute-start(f32[12,8,128]{2,1,0:T(8,128)S(1)} %pad_maximum_fusion.1), channel_id=1, source_target_pairs={{0,16},{16,0},{1,17},{17,1},{2,18},{18,2},{3,19},{19,3},{4,20},{20... | collective-permute-start | bytes 147464 | tf_op jit(solution)/shard_map/ppermute | solution.py:758
  37.8 3.1 %collective-permute-start.14 = (f32[73,8,128]{2,1,0:T(8,128)S(1)}, f32[73,8,128]{2,1,0:T(8,128)S(1)}, u32[]{:S(2)}, u32[]{:S(2)}) collective-permute-start(f32[73,8,128]{2,1,0:T(8,128)S(1)} %dynamic-slice_dynamic-update-slice_fusion), channel_id=1, source_target_pairs={{4,8},{8,4},{5,9},{9,5},{6,10},{10,6},{7,11},{11,7},{20,24},{24,20... | collective-permute-start | bytes 897032 | tf_op jit(solution)/shard_map/ppermute | solution.py:747
  38.5 3.6 %collective-permute-start.13 = (f32[73,8,128]{2,1,0:T(8,128)S(1)}, f32[73,8,128]{2,1,0:T(8,128)S(1)}, u32[]{:S(2)}, u32[]{:S(2)}) collective-permute-start(f32[73,8,128]{2,1,0:T(8,128)S(1)} %dynamic-slice_dynamic-update-slice_fusion.1), channel_id=1, source_target_pairs={{0,4},{8,12},{4,0},{12,8},{1,5},{9,13},{5,1},{13,9},{2,6},{10,14},... | collective-permute-start | bytes 897032 | tf_op jit(solution)/shard_map/ppermute | solution.py:747
